TPU v7x, 512 devices: a whole 4x4x16 slice. The times are simulated.
512 devices in a mesh: level: 8 (over x, core), row: 16 (over z), col: 4 (over y).
Axes of the slice: x: 4, y: 4, z: 16, core: 2. Of those that a mesh axis runs over, the one named last changes fastest.
Arguments:
- factor_tiles: bfloat16 [8, 64, 16, 4, 128, 128], P('level', 'row', None, 'col'), may hold values from -0.0625 to 0.0625
- tile_mask: int32 [8, 64, 16, 4], P('level', 'row', None, 'col'), may hold values from 0 to 1, as said below
- inverse_diagonal: bfloat16 [8, 16, 4, 128, 128], P('level', 'row', 'col'), may hold values from -1.5 to 1.5, as said below
- right_sides: float32 [8, 16, 4, 128, 128], P('level', 'row', 'col'), may hold values from -6 to 6
Outputs:
- forward_solution: bfloat16 [8, 16, 4, 128, 128], P('level', 'row', 'col')
- solution: bfloat16 [8, 16, 4, 128, 128], P('level', 'row', 'col')
Inputs may be any that keep to these rules, and one draw needn't show every extreme that they name: `tile_mask`: 1 where the factor holds the tile, 0 where it does not; tiles are present only where |i - j| <= 32 with j = q * 4 + c, a band that follows the elimination tree. `inverse_diagonal`: each 128 x 128 block is lower triangular, the inverse of a diagonal block of the factor.
All inputs are finite; a program needn't handle non-finite values.
Results may differ from a plain program's by a relative error of at most 0.035.
Values may be sent and summed in bfloat16 or wider, within the bound.
A program may use at most 64 MiB of HBM per device.

v0:
```python
import jax
import jax.numpy as jnp
from jax import lax
from jax.sharding import PartitionSpec as P


def shifted(block, axis, distance):
    devices = range(lax.axis_size(axis))
    route = [(i - distance, i) for i in devices if i - distance in devices]
    return lax.ppermute(block, axis, route)


def solve_block(inverse, values):
    return jnp.einsum(
        "kst,ktr->ksr", inverse, values.astype(jnp.bfloat16), preferred_element_type=jnp.float32
    ).astype(jnp.bfloat16)


def solve_transposed(inverse, values):
    return jnp.einsum(
        "kts,ktr->ksr", inverse, values.astype(jnp.bfloat16), preferred_element_type=jnp.float32
    ).astype(jnp.bfloat16)


def local(factor_tiles, tile_mask, inverse_diagonal, right_sides):
    nlev = lax.axis_size("level")
    ncol = lax.axis_size("col")
    masked = factor_tiles[0, :, :, 0] * tile_mask[0, :, :, 0][:, :, None, None].astype(jnp.bfloat16)
    block_rows = masked.shape[0]
    qcount = masked.shape[1]
    side = masked.shape[2]
    own_rows = block_rows // ncol
    masked_split = masked.reshape(own_rows, ncol, qcount, side, side)
    inverse = inverse_diagonal[0, :, 0]
    sides = right_sides[0, :, 0]
    total_cols = sides.shape[-1]
    width, count, split = (total_cols, nlev - 1, 0)
    solved = solve_block(inverse, sides)
    for step in range(1, count + 1):
        piece = solved
        arrived = shifted(piece, "level", 1)
        partial_value = jnp.einsum(
            "aqst,qtr->asr",
            masked,
            lax.all_gather(arrived, "row", axis=0, tiled=True),
            preferred_element_type=jnp.float32,
        )
        pieces = lax.all_to_all(
            partial_value.reshape(own_rows, ncol, side, width).astype(jnp.bfloat16),
            "col",
            split_axis=1,
            concat_axis=1,
            tiled=True,
        ).astype(jnp.float32)
        mine = jnp.sum(pieces, axis=1)
        source = sides
        solved = solve_block(inverse, source - mine)
    answer = solve_transposed(inverse, solved)
    for step in range(1, count + 1):
        piece = answer[:, None]
        fold_piece = lax.all_gather(piece, "col", axis=1, tiled=True)
        partial_value = jnp.einsum(
            "kcqst,kcsr->qtr", masked_split, fold_piece, preferred_element_type=jnp.float32
        )
        summed = lax.psum_scatter(
            partial_value.astype(jnp.bfloat16), "row", scatter_dimension=0, tiled=True
        ).astype(jnp.float32)
        arrived = shifted(summed.astype(jnp.bfloat16), "level", -1).astype(summed.dtype)
        source = solved.astype(jnp.float32)
        answer = solve_transposed(inverse, source - arrived)
    return (solved[None, :, None], answer[None, :, None])


def solution(mesh):
    placed = (
        P("level", "row", None, "col", None, None),
        P("level", "row", None, "col"),
        P("level", "row", "col", None, None),
        P("level", "row", "col", None, None),
    )
    return jax.shard_map(
        local,
        mesh=mesh,
        in_specs=placed,
        out_specs=(P("level", "row", "col", None, None), P("level", "row", "col", None, None)),
        check_vma=False,
    )
```

profile of v0, /device:TPU:1, one launch (start us, length us, event | category | flops | bytes accessed | tf_op | source)
XLA Modules:
  0.0 923.1 jit_solution(2617397229417016310)
XLA Ops:
  8.9 4.5 collective-permute-start
  14.1 3.6 collective-permute-done
  17.8 28.6 %all_gather.42 = bf16[16,128,128]{2,1,0:T(8,128)(2,1)S(1)} all-gather(bf16[1,128,128]{2,1,0:T(8,128)(2,1)S(1)} %collective-permute-done), channel_id=1, replica_groups=mesh['level'=8,'row'=16,'col'=4] {'row'}, dimensions={0}, use_global_device_ids=true | all-gather | bytes 557056 | tf_op jit(solution)/shard_map/all_gather | solution.py:45
  48.8 8.8 all_to_all.35
  57.9 12.0 %collective-permute-start.1 = (bf16[1,128,128]{1,2,0:T(8,128)(2,1)S(1)}, bf16[1,128,128]{1,2,0:T(8,128)(2,1)S(1)}, u32[]{:S(2)}, u32[]{:S(2)}) collective-permute-start(bf16[1,128,128]{1,2,0:T(8,128)(2,1)S(1)} %fusion.71), channel_id=1, source_target_pairs={{0,64},{64,128},{128,192},{192,256},{256,320},{320,384},{384,448},... | collective-permute-start | bytes 98312 | tf_op jit(solution)/shard_map/ppermute | solution.py:10
  71.0 22.7 %all_gather.43 = bf16[16,128,128]{2,1,0:T(8,128)(2,1)S(1)} all-gather(bf16[1,128,128]{2,1,0:T(8,128)(2,1)S(1)} %copy.36), channel_id=1, replica_groups=mesh['level'=8,'row'=16,'col'=4] {'row'}, dimensions={0}, use_global_device_ids=true | all-gather | bytes 557056 | tf_op jit(solution)/shard_map/all_gather | solution.py:45
  94.4 7.2 all_to_all.36
  101.9 12.0 %collective-permute-start.2 = (bf16[1,128,128]{1,2,0:T(8,128)(2,1)S(1)}, bf16[1,128,128]{1,2,0:T(8,128)(2,1)S(1)}, u32[]{:S(2)}, u32[]{:S(2)}) collective-permute-start(bf16[1,128,128]{1,2,0:T(8,128)(2,1)S(1)} %fusion.72), channel_id=1, source_target_pairs={{0,64},{64,128},{128,192},{192,256},{256,320},{320,384},{384,448},... | collective-permute-start | bytes 98312 | tf_op jit(solution)/shard_map/ppermute | solution.py:10
  115.0 23.8 %all_gather.44 = bf16[16,128,128]{2,1,0:T(8,128)(2,1)S(1)} all-gather(bf16[1,128,128]{2,1,0:T(8,128)(2,1)S(1)} %copy.38), channel_id=1, replica_groups=mesh['level'=8,'row'=16,'col'=4] {'row'}, dimensions={0}, use_global_device_ids=true | all-gather | bytes 557056 | tf_op jit(solution)/shard_map/all_gather | solution.py:45
  139.5 8.1 all_to_all.37
  147.9 11.6 %collective-permute-start.3 = (bf16[1,128,128]{1,2,0:T(8,128)(2,1)S(1)}, bf16[1,128,128]{1,2,0:T(8,128)(2,1)S(1)}, u32[]{:S(2)}, u32[]{:S(2)}) collective-permute-start(bf16[1,128,128]{1,2,0:T(8,128)(2,1)S(1)} %fusion.73), channel_id=1, source_target_pairs={{0,64},{64,128},{128,192},{192,256},{256,320},{320,384},{384,448},... | collective-permute-start | bytes 98312 | tf_op jit(solution)/shard_map/ppermute | solution.py:10
  160.7 22.7 %all_gather.45 = bf16[16,128,128]{2,1,0:T(8,128)(2,1)S(1)} all-gather(bf16[1,128,128]{2,1,0:T(8,128)(2,1)S(1)} %copy.40), channel_id=1, replica_groups=mesh['level'=8,'row'=16,'col'=4] {'row'}, dimensions={0}, use_global_device_ids=true | all-gather | bytes 557056 | tf_op jit(solution)/shard_map/all_gather | solution.py:45
  184.2 7.2 all_to_all.38
  191.6 11.7 %collective-permute-start.4 = (bf16[1,128,128]{1,2,0:T(8,128)(2,1)S(1)}, bf16[1,128,128]{1,2,0:T(8,128)(2,1)S(1)}, u32[]{:S(2)}, u32[]{:S(2)}) collective-permute-start(bf16[1,128,128]{1,2,0:T(8,128)(2,1)S(1)} %fusion.74), channel_id=1, source_target_pairs={{0,64},{64,128},{128,192},{192,256},{256,320},{320,384},{384,448},... | collective-permute-start | bytes 98312 | tf_op jit(solution)/shard_map/ppermute | solution.py:10
  204.4 23.7 %all_gather.46 = bf16[16,128,128]{2,1,0:T(8,128)(2,1)S(1)} all-gather(bf16[1,128,128]{2,1,0:T(8,128)(2,1)S(1)} %copy.42), channel_id=1, replica_groups=mesh['level'=8,'row'=16,'col'=4] {'row'}, dimensions={0}, use_global_device_ids=true | all-gather | bytes 557056 | tf_op jit(solution)/shard_map/all_gather | solution.py:45
  228.8 7.2 all_to_all.39
  236.2 12.5 %collective-permute-start.5 = (bf16[1,128,128]{1,2,0:T(8,128)(2,1)S(1)}, bf16[1,128,128]{1,2,0:T(8,128)(2,1)S(1)}, u32[]{:S(2)}, u32[]{:S(2)}) collective-permute-start(bf16[1,128,128]{1,2,0:T(8,128)(2,1)S(1)} %fusion.75), channel_id=1, source_target_pairs={{0,64},{64,128},{128,192},{192,256},{256,320},{320,384},{384,448},... | collective-permute-start | bytes 98312 | tf_op jit(solution)/shard_map/ppermute | solution.py:10
  249.8 22.7 %all_gather.47 = bf16[16,128,128]{2,1,0:T(8,128)(2,1)S(1)} all-gather(bf16[1,128,128]{2,1,0:T(8,128)(2,1)S(1)} %copy.44), channel_id=1, replica_groups=mesh['level'=8,'row'=16,'col'=4] {'row'}, dimensions={0}, use_global_device_ids=true | all-gather | bytes 557056 | tf_op jit(solution)/shard_map/all_gather | solution.py:45
  273.3 7.2 all_to_all.40
  280.8 12.4 %collective-permute-start.6 = (bf16[1,128,128]{1,2,0:T(8,128)(2,1)S(1)}, bf16[1,128,128]{1,2,0:T(8,128)(2,1)S(1)}, u32[]{:S(2)}, u32[]{:S(2)}) collective-permute-start(bf16[1,128,128]{1,2,0:T(8,128)(2,1)S(1)} %fusion.76), channel_id=1, source_target_pairs={{0,64},{64,128},{128,192},{192,256},{256,320},{320,384},{384,448},... | collective-permute-start | bytes 98312 | tf_op jit(solution)/shard_map/ppermute | solution.py:10
  294.2 23.5 %all_gather.48 = bf16[16,128,128]{2,1,0:T(8,128)(2,1)S(1)} all-gather(bf16[1,128,128]{2,1,0:T(8,128)(2,1)S(1)} %copy.46), channel_id=1, replica_groups=mesh['level'=8,'row'=16,'col'=4] {'row'}, dimensions={0}, use_global_device_ids=true | all-gather | bytes 557056 | tf_op jit(solution)/shard_map/all_gather | solution.py:45
  318.5 7.2 all_to_all.41
  326.1 8.5 all-gather
  336.1 64.7 %reduce-scatter.8.cloned.1.call-done = bf16[1,128,128]{1,2,0:T(8,128)(2,1)} async-done(((bf16[16,128,128]{1,2,0:T(8,128)(2,1)}), bf16[1,128,128]{1,2,0:T(8,128)(2,1)}) %reduce-scatter.8.cloned.1.call-update) | async-done | bytes 32784 | tf_op jit(solution)/shard_map/reduce_scatter | solution.py:65
  400.8 13.2 %collective-permute-start.7 = (bf16[1,128,128]{1,2,0:T(8,128)(2,1)}, bf16[1,128,128]{1,2,0:T(8,128)(2,1)S(1)}, u32[]{:S(2)}, u32[]{:S(2)}) collective-permute-start(bf16[1,128,128]{1,2,0:T(8,128)(2,1)} %reduce-scatter.8.cloned.1.call-done), channel_id=1, source_target_pairs={{64,0},{128,64},{192,128},{256,192},{320,256},{384,320},{448,384},... | collective-permute-start | bytes 98312 | tf_op jit(solution)/shard_map/ppermute | solution.py:10
  414.0 2.9 collective-permute-done.7
  417.0 9.4 %all-gather.1 = bf16[512,128]{0,1:T(8,128)(2,1)S(1)} all-gather(bf16[128,128]{0,1:T(8,128)(2,1)S(1)} %fusion.78), channel_id=3, replica_groups=mesh['level'=8,'row'=16,'col'=4] {'col'}, dimensions={0}, use_global_device_ids=true | all-gather | bytes 163840 | tf_op jit(solution)/shard_map/all_gather | solution.py:61
  427.9 55.9 %reduce-scatter.10.cloned.1.call-done = bf16[1,128,128]{1,2,0:T(8,128)(2,1)} async-done(((bf16[16,128,128]{1,2,0:T(8,128)(2,1)}), bf16[1,128,128]{1,2,0:T(8,128)(2,1)}) %reduce-scatter.10.cloned.1.call-update) | async-done | bytes 32784 | tf_op jit(solution)/shard_map/reduce_scatter | solution.py:65
  483.8 13.3 %collective-permute-start.8 = (bf16[1,128,128]{1,2,0:T(8,128)(2,1)}, bf16[1,128,128]{1,2,0:T(8,128)(2,1)S(1)}, u32[]{:S(2)}, u32[]{:S(2)}) collective-permute-start(bf16[1,128,128]{1,2,0:T(8,128)(2,1)} %reduce-scatter.10.cloned.1.call-done), channel_id=1, source_target_pairs={{64,0},{128,64},{192,128},{256,192},{320,256},{384,320},{448,384},... | collective-permute-start | bytes 98312 | tf_op jit(solution)/shard_map/ppermute | solution.py:10
  497.1 2.8 collective-permute-done.8
  500.0 9.4 %all-gather.2 = bf16[512,128]{0,1:T(8,128)(2,1)S(1)} all-gather(bf16[128,128]{0,1:T(8,128)(2,1)S(1)} %fusion.79), channel_id=4, replica_groups=mesh['level'=8,'row'=16,'col'=4] {'col'}, dimensions={0}, use_global_device_ids=true | all-gather | bytes 163840 | tf_op jit(solution)/shard_map/all_gather | solution.py:61
  511.0 55.9 %reduce-scatter.12.cloned.1.call-done = bf16[1,128,128]{1,2,0:T(8,128)(2,1)} async-done(((bf16[16,128,128]{1,2,0:T(8,128)(2,1)}), bf16[1,128,128]{1,2,0:T(8,128)(2,1)}) %reduce-scatter.12.cloned.1.call-update) | async-done | bytes 32784 | tf_op jit(solution)/shard_map/reduce_scatter | solution.py:65
  566.9 13.2 %collective-permute-start.9 = (bf16[1,128,128]{1,2,0:T(8,128)(2,1)}, bf16[1,128,128]{1,2,0:T(8,128)(2,1)S(1)}, u32[]{:S(2)}, u32[]{:S(2)}) collective-permute-start(bf16[1,128,128]{1,2,0:T(8,128)(2,1)} %reduce-scatter.12.cloned.1.call-done), channel_id=1, source_target_pairs={{64,0},{128,64},{192,128},{256,192},{320,256},{384,320},{448,384},... | collective-permute-start | bytes 98312 | tf_op jit(solution)/shard_map/ppermute | solution.py:10
  580.1 2.9 collective-permute-done.9
  583.1 9.4 %all-gather.3 = bf16[512,128]{0,1:T(8,128)(2,1)S(1)} all-gather(bf16[128,128]{0,1:T(8,128)(2,1)S(1)} %fusion.80), channel_id=5, replica_groups=mesh['level'=8,'row'=16,'col'=4] {'col'}, dimensions={0}, use_global_device_ids=true | all-gather | bytes 163840 | tf_op jit(solution)/shard_map/all_gather | solution.py:61
  594.1 55.3 %reduce-scatter.14.cloned.1.call-done = bf16[1,128,128]{1,2,0:T(8,128)(2,1)} async-done(((bf16[16,128,128]{1,2,0:T(8,128)(2,1)}), bf16[1,128,128]{1,2,0:T(8,128)(2,1)}) %reduce-scatter.14.cloned.1.call-update) | async-done | bytes 32784 | tf_op jit(solution)/shard_map/reduce_scatter | solution.py:65
  649.4 13.9 %collective-permute-start.10 = (bf16[1,128,128]{1,2,0:T(8,128)(2,1)}, bf16[1,128,128]{1,2,0:T(8,128)(2,1)S(1)}, u32[]{:S(2)}, u32[]{:S(2)}) collective-permute-start(bf16[1,128,128]{1,2,0:T(8,128)(2,1)} %reduce-scatter.14.cloned.1.call-done), channel_id=1, source_target_pairs={{64,0},{128,64},{192,128},{256,192},{320,256},{384,320},{448,384},... | collective-permute-start | bytes 98312 | tf_op jit(solution)/shard_map/ppermute | solution.py:10
  666.2 9.5 %all-gather.4 = bf16[512,128]{0,1:T(8,128)(2,1)S(1)} all-gather(bf16[128,128]{0,1:T(8,128)(2,1)S(1)} %fusion.81), channel_id=6, replica_groups=mesh['level'=8,'row'=16,'col'=4] {'col'}, dimensions={0}, use_global_device_ids=true | all-gather | bytes 163840 | tf_op jit(solution)/shard_map/all_gather | solution.py:61
  677.2 55.5 %reduce-scatter.16.cloned.1.call-done = bf16[1,128,128]{1,2,0:T(8,128)(2,1)} async-done(((bf16[16,128,128]{1,2,0:T(8,128)(2,1)}), bf16[1,128,128]{1,2,0:T(8,128)(2,1)}) %reduce-scatter.16.cloned.1.call-update) | async-done | bytes 32784 | tf_op jit(solution)/shard_map/reduce_scatter | solution.py:65
  732.8 13.6 %collective-permute-start.11 = (bf16[1,128,128]{1,2,0:T(8,128)(2,1)}, bf16[1,128,128]{1,2,0:T(8,128)(2,1)S(1)}, u32[]{:S(2)}, u32[]{:S(2)}) collective-permute-start(bf16[1,128,128]{1,2,0:T(8,128)(2,1)} %reduce-scatter.16.cloned.1.call-done), channel_id=1, source_target_pairs={{64,0},{128,64},{192,128},{256,192},{320,256},{384,320},{448,384},... | collective-permute-start | bytes 98312 | tf_op jit(solution)/shard_map/ppermute | solution.py:10
  746.4 2.9 collective-permute-done.11
  749.4 9.5 %all-gather.5 = bf16[512,128]{0,1:T(8,128)(2,1)S(1)} all-gather(bf16[128,128]{0,1:T(8,128)(2,1)S(1)} %fusion.82), channel_id=7, replica_groups=mesh['level'=8,'row'=16,'col'=4] {'col'}, dimensions={0}, use_global_device_ids=true | all-gather | bytes 163840 | tf_op jit(solution)/shard_map/all_gather | solution.py:61
  760.4 55.8 %reduce-scatter.18.cloned.1.call-done = bf16[1,128,128]{1,2,0:T(8,128)(2,1)} async-done(((bf16[16,128,128]{1,2,0:T(8,128)(2,1)}), bf16[1,128,128]{1,2,0:T(8,128)(2,1)}) %reduce-scatter.18.cloned.1.call-update) | async-done | bytes 32784 | tf_op jit(solution)/shard_map/reduce_scatter | solution.py:65
  816.2 13.2 %collective-permute-start.12 = (bf16[1,128,128]{1,2,0:T(8,128)(2,1)}, bf16[1,128,128]{1,2,0:T(8,128)(2,1)S(1)}, u32[]{:S(2)}, u32[]{:S(2)}) collective-permute-start(bf16[1,128,128]{1,2,0:T(8,128)(2,1)} %reduce-scatter.18.cloned.1.call-done), channel_id=1, source_target_pairs={{64,0},{128,64},{192,128},{256,192},{320,256},{384,320},{448,384},... | collective-permute-start | bytes 98312 | tf_op jit(solution)/shard_map/ppermute | solution.py:10
  829.4 2.9 collective-permute-done.12
  832.4 9.5 %all-gather.6 = bf16[512,128]{0,1:T(8,128)(2,1)S(1)} all-gather(bf16[128,128]{0,1:T(8,128)(2,1)S(1)} %fusion.83), channel_id=8, replica_groups=mesh['level'=8,'row'=16,'col'=4] {'col'}, dimensions={0}, use_global_device_ids=true | all-gather | bytes 163840 | tf_op jit(solution)/shard_map/all_gather | solution.py:61
  843.4 55.8 %reduce-scatter.20.cloned.1.call-done = bf16[1,128,128]{1,2,0:T(8,128)(2,1)} async-done(((bf16[16,128,128]{1,2,0:T(8,128)(2,1)}), bf16[1,128,128]{1,2,0:T(8,128)(2,1)}) %reduce-scatter.20.cloned.1.call-update) | async-done | bytes 32784 | tf_op jit(solution)/shard_map/reduce_scatter | solution.py:65
  899.2 13.2 %collective-permute-start.13 = (bf16[1,128,128]{1,2,0:T(8,128)(2,1)}, bf16[1,128,128]{1,2,0:T(8,128)(2,1)S(1)}, u32[]{:S(2)}, u32[]{:S(2)}) collective-permute-start(bf16[1,128,128]{1,2,0:T(8,128)(2,1)} %reduce-scatter.20.cloned.1.call-done), channel_id=1, source_target_pairs={{64,0},{128,64},{192,128},{256,192},{320,256},{384,320},{448,384},... | collective-permute-start | bytes 98312 | tf_op jit(solution)/shard_map/ppermute | solution.py:10
  (82 shorter events, 35.5 us)
Async XLA Ops:
  7.2 0.8 copy-start
  7.2 393.6 %reduce-scatter.8.cloned.1.call-start = ((), (), s32[]{:S(2)}) async-start(), calls=%async_computation.14 | async-start | bytes 557056 | tf_op jit(solution)/shard_map/reduce_scatter | solution.py:65
  8.9 8.9 collective-permute-start
  46.3 11.3 %copy-start.1 = (f32[1,1,1,128,128]{4,3,2,1,0:T(8,128)S(1)}, f32[1,1,1,128,128]{4,3,2,1,0:T(8,128)}, u32[]{:S(2)}) copy-start(f32[1,1,1,128,128]{4,3,2,1,0:T(8,128)} %param.7) | copy-start | bytes 196612
  46.3 47.4 %copy-start.2 = (bf16[1,4,16,1,128,128]{5,4,3,2,1,0:T(8,128)(2,1)S(1)}, bf16[1,4,16,1,128,128]{5,4,3,2,1,0:T(8,128)(2,1)}, u32[]{:S(2)}) copy-start(bf16[1,4,16,1,128,128]{5,4,3,2,1,0:T(8,128)(2,1)} %param.4) | copy-start | bytes 6291460
  57.9 13.0 %collective-permute-start.1 = (bf16[1,128,128]{1,2,0:T(8,128)(2,1)S(1)}, bf16[1,128,128]{1,2,0:T(8,128)(2,1)S(1)}, u32[]{:S(2)}, u32[]{:S(2)}) collective-permute-start(bf16[1,128,128]{1,2,0:T(8,128)(2,1)S(1)} %fusion.71), channel_id=1, source_target_pairs={{0,64},{64,128},{128,192},{192,256},{256,320},{320,384},{384,448},... | collective-permute-start | bytes 98312 | tf_op jit(solution)/shard_map/ppermute | solution.py:10
  101.9 13.0 %collective-permute-start.2 = (bf16[1,128,128]{1,2,0:T(8,128)(2,1)S(1)}, bf16[1,128,128]{1,2,0:T(8,128)(2,1)S(1)}, u32[]{:S(2)}, u32[]{:S(2)}) collective-permute-start(bf16[1,128,128]{1,2,0:T(8,128)(2,1)S(1)} %fusion.72), channel_id=1, source_target_pairs={{0,64},{64,128},{128,192},{192,256},{256,320},{320,384},{384,448},... | collective-permute-start | bytes 98312 | tf_op jit(solution)/shard_map/ppermute | solution.py:10
  147.9 12.6 %collective-permute-start.3 = (bf16[1,128,128]{1,2,0:T(8,128)(2,1)S(1)}, bf16[1,128,128]{1,2,0:T(8,128)(2,1)S(1)}, u32[]{:S(2)}, u32[]{:S(2)}) collective-permute-start(bf16[1,128,128]{1,2,0:T(8,128)(2,1)S(1)} %fusion.73), channel_id=1, source_target_pairs={{0,64},{64,128},{128,192},{192,256},{256,320},{320,384},{384,448},... | collective-permute-start | bytes 98312 | tf_op jit(solution)/shard_map/ppermute | solution.py:10
  191.6 12.7 %collective-permute-start.4 = (bf16[1,128,128]{1,2,0:T(8,128)(2,1)S(1)}, bf16[1,128,128]{1,2,0:T(8,128)(2,1)S(1)}, u32[]{:S(2)}, u32[]{:S(2)}) collective-permute-start(bf16[1,128,128]{1,2,0:T(8,128)(2,1)S(1)} %fusion.74), channel_id=1, source_target_pairs={{0,64},{64,128},{128,192},{192,256},{256,320},{320,384},{384,448},... | collective-permute-start | bytes 98312 | tf_op jit(solution)/shard_map/ppermute | solution.py:10
  236.2 13.5 %collective-permute-start.5 = (bf16[1,128,128]{1,2,0:T(8,128)(2,1)S(1)}, bf16[1,128,128]{1,2,0:T(8,128)(2,1)S(1)}, u32[]{:S(2)}, u32[]{:S(2)}) collective-permute-start(bf16[1,128,128]{1,2,0:T(8,128)(2,1)S(1)} %fusion.75), channel_id=1, source_target_pairs={{0,64},{64,128},{128,192},{192,256},{256,320},{320,384},{384,448},... | collective-permute-start | bytes 98312 | tf_op jit(solution)/shard_map/ppermute | solution.py:10
  280.8 13.4 %collective-permute-start.6 = (bf16[1,128,128]{1,2,0:T(8,128)(2,1)S(1)}, bf16[1,128,128]{1,2,0:T(8,128)(2,1)S(1)}, u32[]{:S(2)}, u32[]{:S(2)}) collective-permute-start(bf16[1,128,128]{1,2,0:T(8,128)(2,1)S(1)} %fusion.76), channel_id=1, source_target_pairs={{0,64},{64,128},{128,192},{192,256},{256,320},{320,384},{384,448},... | collective-permute-start | bytes 98312 | tf_op jit(solution)/shard_map/ppermute | solution.py:10
  336.0 147.8 %reduce-scatter.10.cloned.1.call-start = ((), (), s32[]{:S(2)}) async-start(), calls=%async_computation.15 | async-start | bytes 557056 | tf_op jit(solution)/shard_map/reduce_scatter | solution.py:65
  400.8 16.1 %collective-permute-start.7 = (bf16[1,128,128]{1,2,0:T(8,128)(2,1)}, bf16[1,128,128]{1,2,0:T(8,128)(2,1)S(1)}, u32[]{:S(2)}, u32[]{:S(2)}) collective-permute-start(bf16[1,128,128]{1,2,0:T(8,128)(2,1)} %reduce-scatter.8.cloned.1.call-done), channel_id=1, source_target_pairs={{64,0},{128,64},{192,128},{256,192},{320,256},{384,320},{448,384},... | collective-permute-start | bytes 98312 | tf_op jit(solution)/shard_map/ppermute | solution.py:10
  427.9 139.0 %reduce-scatter.12.cloned.1.call-start = ((), (), s32[]{:S(2)}) async-start(), calls=%async_computation.16 | async-start | bytes 557056 | tf_op jit(solution)/shard_map/reduce_scatter | solution.py:65
  483.8 16.1 %collective-permute-start.8 = (bf16[1,128,128]{1,2,0:T(8,128)(2,1)}, bf16[1,128,128]{1,2,0:T(8,128)(2,1)S(1)}, u32[]{:S(2)}, u32[]{:S(2)}) collective-permute-start(bf16[1,128,128]{1,2,0:T(8,128)(2,1)} %reduce-scatter.10.cloned.1.call-done), channel_id=1, source_target_pairs={{64,0},{128,64},{192,128},{256,192},{320,256},{384,320},{448,384},... | collective-permute-start | bytes 98312 | tf_op jit(solution)/shard_map/ppermute | solution.py:10
  510.9 138.5 %reduce-scatter.14.cloned.1.call-start = ((), (), s32[]{:S(2)}) async-start(), calls=%async_computation.17 | async-start | bytes 557056 | tf_op jit(solution)/shard_map/reduce_scatter | solution.py:65
  566.9 16.1 %collective-permute-start.9 = (bf16[1,128,128]{1,2,0:T(8,128)(2,1)}, bf16[1,128,128]{1,2,0:T(8,128)(2,1)S(1)}, u32[]{:S(2)}, u32[]{:S(2)}) collective-permute-start(bf16[1,128,128]{1,2,0:T(8,128)(2,1)} %reduce-scatter.12.cloned.1.call-done), channel_id=1, source_target_pairs={{64,0},{128,64},{192,128},{256,192},{320,256},{384,320},{448,384},... | collective-permute-start | bytes 98312 | tf_op jit(solution)/shard_map/ppermute | solution.py:10
  594.0 138.7 %reduce-scatter.16.cloned.1.call-start = ((), (), s32[]{:S(2)}) async-start(), calls=%async_computation.18 | async-start | bytes 557056 | tf_op jit(solution)/shard_map/reduce_scatter | solution.py:65
  649.4 16.7 %collective-permute-start.10 = (bf16[1,128,128]{1,2,0:T(8,128)(2,1)}, bf16[1,128,128]{1,2,0:T(8,128)(2,1)S(1)}, u32[]{:S(2)}, u32[]{:S(2)}) collective-permute-start(bf16[1,128,128]{1,2,0:T(8,128)(2,1)} %reduce-scatter.14.cloned.1.call-done), channel_id=1, source_target_pairs={{64,0},{128,64},{192,128},{256,192},{320,256},{384,320},{448,384},... | collective-permute-start | bytes 98312 | tf_op jit(solution)/shard_map/ppermute | solution.py:10
  677.2 139.0 %reduce-scatter.18.cloned.1.call-start = ((), (), s32[]{:S(2)}) async-start(), calls=%async_computation.19 | async-start | bytes 557056 | tf_op jit(solution)/shard_map/reduce_scatter | solution.py:65
  732.8 16.5 %collective-permute-start.11 = (bf16[1,128,128]{1,2,0:T(8,128)(2,1)}, bf16[1,128,128]{1,2,0:T(8,128)(2,1)S(1)}, u32[]{:S(2)}, u32[]{:S(2)}) collective-permute-start(bf16[1,128,128]{1,2,0:T(8,128)(2,1)} %reduce-scatter.16.cloned.1.call-done), channel_id=1, source_target_pairs={{64,0},{128,64},{192,128},{256,192},{320,256},{384,320},{448,384},... | collective-permute-start | bytes 98312 | tf_op jit(solution)/shard_map/ppermute | solution.py:10
  760.4 138.8 %reduce-scatter.20.cloned.1.call-start = ((), (), s32[]{:S(2)}) async-start(), calls=%async_computation.20 | async-start | bytes 557056 | tf_op jit(solution)/shard_map/reduce_scatter | solution.py:65
  816.2 16.1 %collective-permute-start.12 = (bf16[1,128,128]{1,2,0:T(8,128)(2,1)}, bf16[1,128,128]{1,2,0:T(8,128)(2,1)S(1)}, u32[]{:S(2)}, u32[]{:S(2)}) collective-permute-start(bf16[1,128,128]{1,2,0:T(8,128)(2,1)} %reduce-scatter.18.cloned.1.call-done), channel_id=1, source_target_pairs={{64,0},{128,64},{192,128},{256,192},{320,256},{384,320},{448,384},... | collective-permute-start | bytes 98312 | tf_op jit(solution)/shard_map/ppermute | solution.py:10
  899.2 16.2 %collective-permute-start.13 = (bf16[1,128,128]{1,2,0:T(8,128)(2,1)}, bf16[1,128,128]{1,2,0:T(8,128)(2,1)S(1)}, u32[]{:S(2)}, u32[]{:S(2)}) collective-permute-start(bf16[1,128,128]{1,2,0:T(8,128)(2,1)} %reduce-scatter.20.cloned.1.call-done), channel_id=1, source_target_pairs={{64,0},{128,64},{192,128},{256,192},{320,256},{384,320},{448,384},... | collective-permute-start | bytes 98312 | tf_op jit(solution)/shard_map/ppermute | solution.py:10
Sparse Core Ops, SparseCore 0:
  336.1 64.5 reduce-scatter.7
  428.0 55.7 reduce-scatter.9
  511.0 55.7 reduce-scatter.11
  594.1 55.2 reduce-scatter.13
  677.3 55.4 reduce-scatter.15
  760.5 55.6 reduce-scatter.17
  843.5 55.6 reduce-scatter.19
where the time goes:
time: 924 us; the launch traced here: 923 us
  waiting for transfers between devices  428 us (46%)
  blocking collectives  286 us (31%)
  starting transfers between devices  170 us (18%)
  matrix products  19.6 us (2%)
  between operations  14.5 us (2%)
    reduce_scatter x7, waiting for transfers between devices, local(): lax.psum_scatter(partial_value.astype(jnp.bfloat16), 'row', scatter_dimen...  399 us
    ppermute x14, starting transfers between devices, shifted(): return lax.ppermute(block, axis, route)  170 us
    all_gather x7, blocking collectives, local(): lax.all_gather(arrived, 'row', axis=0, tiled=True)  168 us
    all_gather x7, blocking collectives, local(): fold_piece = lax.all_gather(piece, 'col', axis=1, tiled=True)  65.2 us
    all_to_all x7, blocking collectives, local(): lax.all_to_all(partial_value.reshape(own_rows, ncol, side, width).astype(...  53 us
    ppermute x14, waiting for transfers between devices, shifted(): return lax.ppermute(block, axis, route)  29.1 us
  transfers between devices with their start and end apart: 21, of which 21 were waited for; matrix products, arithmetic and copies ran while one was open for 0% of the time, Pallas kernels for 0%

commit v1 on v0

v1 whole, which is shorter than its diff:
```python
import functools

import jax
import jax.numpy as jnp
from jax import lax
from jax.experimental import pallas as pl
from jax.experimental.pallas import tpu as pltpu
from jax.sharding import PartitionSpec as P

MESH = pl.DeviceIdType.MESH
BAND = 8
FAR_FIRST = sorted(range(-BAND, BAND + 1), key=lambda d: -abs(d))


def kernel(
    nlev, nrow, ncol, chunks,
    tiles_ref, mask_ref, inverse_ref, sides_ref,
    forward_ref, answer_ref,
    wf, wb, inv_t, sides_t,
    xin, part, part_f, yin, ysol, xsol, bin_, zout, zin, update,
    fz_send, fz_recv, fy_send, fy_recv, by_send, by_recv, bz_send, bz_recv,
):
    l, z, c = lax.axis_index("level"), lax.axis_index("row"), lax.axis_index("col")
    rows = sides_ref.shape[0] // chunks
    side = sides_ref.shape[0]
    last = nlev - 1
    others = [lax.rem(c + o, ncol) for o in range(1, ncol)]

    for q in range(nrow):
        @pl.when((q - z > BAND) | (z - q > BAND))
        def _():
            for k in range(chunks):
                xin[k, q] = jnp.zeros_like(xin[k, q])
                zin[k, q] = jnp.zeros_like(zin[k, q])

    barrier = pltpu.get_barrier_semaphore()
    for o in others:
        pl.semaphore_signal(barrier, inc=1, device_id=(l, z, o), device_id_type=MESH)

    @pl.when(l < last)
    def _():
        for q in range(nrow):
            pl.semaphore_signal(barrier, inc=1, device_id=(l + 1, q, c), device_id_type=MESH)

    @pl.when(l > 0)
    def _():
        for q in range(nrow):
            pl.semaphore_signal(barrier, inc=1, device_id=(l - 1, q, c), device_id_type=MESH)

    inv_t[...] = inverse_ref[...].T
    turned = sides_ref[...].T
    for k in range(chunks):
        sides_t[k] = turned[k * rows:(k + 1) * rows]
    update[...] = jnp.zeros_like(update)

    @pl.when(l > 0)
    def _():
        def prepare(q, carry):
            for a in range(ncol):
                present = mask_ref[a, q].astype(jnp.float32)
                tile = tiles_ref[a, q] * present.astype(jnp.bfloat16)
                wb[q, a * side:(a + 1) * side, :] = tile
                wf[q, :, a * side:(a + 1) * side] = tile.T
            return carry
        lax.fori_loop(0, nrow, prepare, 0)

    pl.semaphore_wait(
        barrier,
        (ncol - 1) + jnp.where(l > 0, nrow, 0) + jnp.where(l < last, nrow, 0),
    )

    def forward_copy(k, q):
        return pltpu.make_async_remote_copy(
            ysol.at[k], xin.at[k, z], fz_send.at[k, q], fz_recv.at[k, z],
            device_id=(l + 1, q, c), device_id_type=MESH)

    def backward_copy(k, q):
        return pltpu.make_async_remote_copy(
            zout.at[k, q], zin.at[k, z], bz_send.at[k, q], bz_recv.at[k, z],
            device_id=(l - 1, q, c), device_id_type=MESH)

    def part_copy(k, o):
        return pltpu.make_async_remote_copy(
            part.at[k, o], yin.at[k, c], fy_send.at[k, o], fy_recv.at[k, c],
            device_id=(l, z, o), device_id_type=MESH)

    def answer_copy(k, o):
        return pltpu.make_async_remote_copy(
            xsol.at[k], bin_.at[k, c], by_send.at[k, o], by_recv.at[k, c],
            device_id=(l, z, o), device_id_type=MESH)

    def arrived(dst, sem):
        pltpu.make_async_copy(dst, dst, sem).wait()

    def in_band(q):
        return (q - z <= BAND) & (z - q <= BAND)

    def forward_step(k):
        @pl.when(l > 0)
        def _():
            for q in range(nrow):
                @pl.when(in_band(q))
                def _():
                    arrived(xin.at[k, q], fz_recv.at[k, q])
            wide = jnp.concatenate([xin[k, q] for q in range(nrow)], axis=1)
            total = jnp.dot(
                wide, wf[...].reshape(nrow * side, ncol * side),
                preferred_element_type=jnp.float32)
            for a in range(ncol):
                piece = total[:, a * side:(a + 1) * side]
                part_f[a] = piece
                part[k, a] = piece.astype(jnp.bfloat16)
            for o in others:
                part_copy(k, o).start()
            for o in others:
                arrived(yin.at[k, o], fy_recv.at[k, o])
            mine = part_f[c]
            for o in others:
                mine = mine + yin[k, o].astype(jnp.float32)
            update[...] = mine

        values = (sides_t[k] - update[...]).astype(jnp.bfloat16)
        ysol[k] = jnp.dot(
            values, inv_t[...], preferred_element_type=jnp.float32).astype(jnp.bfloat16)

        @pl.when(l < last)
        def _():
            for d in FAR_FIRST:
                @pl.when((z + d >= 0) & (z + d < nrow))
                def _():
                    forward_copy(k, z + d).start()

    def backward_step(k):
        @pl.when(l < last)
        def _():
            for q in range(nrow):
                @pl.when(in_band(q))
                def _():
                    arrived(zin.at[k, q], bz_recv.at[k, q])
            update[...] = functools.reduce(
                jnp.add, [zin[k, q].astype(jnp.float32) for q in range(nrow)])

        @pl.when(l == last)
        def _():
            update[...] = jnp.zeros_like(update)

        values = (ysol[k].astype(jnp.float32) - update[...]).astype(jnp.bfloat16)
        xsol[k] = jnp.dot(
            values, inverse_ref[...], preferred_element_type=jnp.float32).astype(jnp.bfloat16)

        @pl.when(l > 0)
        def _():
            for o in others:
                answer_copy(k, o).start()
            bin_[k, c] = xsol[k]
            for o in others:
                arrived(bin_.at[k, o], by_recv.at[k, o])
            wide = jnp.concatenate([bin_[k, a] for a in range(ncol)], axis=1)
            for d in FAR_FIRST:
                @pl.when((z + d >= 0) & (z + d < nrow))
                def _():
                    zout[k, z + d] = jnp.dot(
                        wide, wb[z + d], preferred_element_type=jnp.float32
                    ).astype(jnp.bfloat16)
                    backward_copy(k, z + d).start()

    def forward_sent(k):
        @pl.when(l > 0)
        def _():
            for o in others:
                part_copy(k, o).wait_send()

        @pl.when(l < last)
        def _():
            for d in FAR_FIRST:
                @pl.when((z + d >= 0) & (z + d < nrow))
                def _():
                    forward_copy(k, z + d).wait_send()

    def backward_sent(k):
        @pl.when(l > 0)
        def _():
            for o in others:
                answer_copy(k, o).wait_send()
            for d in FAR_FIRST:
                @pl.when((z + d >= 0) & (z + d < nrow))
                def _():
                    backward_copy(k, z + d).wait_send()

    def step(t, carry):
        at_last = l == last
        is_forward = jnp.where(at_last, lax.rem(t, 2) == 0, t < chunks)
        k = jnp.where(at_last, t // 2, lax.rem(t, chunks))

        @pl.when(is_forward)
        def _():
            forward_step(k)

        @pl.when(t == chunks)
        def _():
            @pl.when(l < last)
            def _():
                lax.fori_loop(0, chunks, lambda j, x: (forward_sent(j), x)[1], 0)

        @pl.when(jnp.logical_not(is_forward))
        def _():
            backward_step(k)

        return carry

    lax.fori_loop(0, 2 * chunks, step, 0)

    @pl.when(l == last)
    def _():
        lax.fori_loop(0, chunks, lambda j, x: (forward_sent(j), x)[1], 0)

    lax.fori_loop(0, chunks, lambda j, x: (backward_sent(j), x)[1], 0)
    for k in range(chunks):
        forward_ref[k * rows:(k + 1) * rows] = ysol[k]
        answer_ref[k * rows:(k + 1) * rows] = xsol[k]


def local(factor_tiles, tile_mask, inverse_diagonal, right_sides):
    nlev, nrow, ncol = (lax.axis_size(n) for n in ("level", "row", "col"))
    tiles = factor_tiles[0, :, :, 0]
    mask = tile_mask[0, :, :, 0]
    inverse = inverse_diagonal[0, 0, 0]
    sides = right_sides[0, 0, 0]
    side, width = sides.shape
    chunks = 4
    rows = width // chunks
    bf16, f32 = jnp.bfloat16, jnp.float32
    vmem = pl.BlockSpec(memory_space=pltpu.VMEM)
    dma = pltpu.SemaphoreType.DMA
    forward, answer = pl.pallas_call(
        functools.partial(kernel, nlev, nrow, ncol, chunks),
        name="levels",
        out_shape=[jax.ShapeDtypeStruct((width, side), bf16)] * 2,
        in_specs=[vmem, pl.BlockSpec(memory_space=pltpu.SMEM), vmem, vmem],
        out_specs=[vmem, vmem],
        scratch_shapes=[
            pltpu.VMEM((nrow, side, ncol * side), bf16),
            pltpu.VMEM((nrow, ncol * side, side), bf16),
            pltpu.VMEM((side, side), bf16),
            pltpu.VMEM((chunks, rows, side), f32),
            pltpu.VMEM((chunks, nrow, rows, side), bf16),
            pltpu.VMEM((chunks, ncol, rows, side), bf16),
            pltpu.VMEM((ncol, rows, side), f32),
            pltpu.VMEM((chunks, ncol, rows, side), bf16),
            pltpu.VMEM((chunks, rows, side), bf16),
            pltpu.VMEM((chunks, rows, side), bf16),
            pltpu.VMEM((chunks, ncol, rows, side), bf16),
            pltpu.VMEM((chunks, nrow, rows, side), bf16),
            pltpu.VMEM((chunks, nrow, rows, side), bf16),
            pltpu.VMEM((rows, side), f32),
            dma((chunks, nrow)), dma((chunks, nrow)),
            dma((chunks, ncol)), dma((chunks, ncol)),
            dma((chunks, ncol)), dma((chunks, ncol)),
            dma((chunks, nrow)), dma((chunks, nrow)),
        ],
        compiler_params=pltpu.CompilerParams(
            collective_id=0, has_side_effects=True, vmem_limit_bytes=40 * 2**20),
        cost_estimate=pl.CostEstimate(flops=2**30, bytes_accessed=2**22, transcendentals=0),
    )(tiles, mask, inverse, sides)
    return (forward.T[None, None, None], answer.T[None, None, None])


def solution(mesh):
    placed = (
        P("level", "row", None, "col", None, None),
        P("level", "row", None, "col"),
        P("level", "row", "col", None, None),
        P("level", "row", "col", None, None),
    )
    return jax.shard_map(
        local,
        mesh=mesh,
        in_specs=placed,
        out_specs=(P("level", "row", "col", None, None), P("level", "row", "col", None, None)),
        check_vma=False,
    )
```

time: 924 us -> 206 us (0.22)
  the two profiles are of different devices: /device:TPU:1 before, /device:TPU:32 now
where the time goes in v1:
time: 206 us
  Pallas kernels  200 us (97%)
  local copies, waits for them, and re-layouts  5.31 us (3%)
    pallas_call x1, Pallas kernels, local(): pl.pallas_call(functools.partial(kernel, nlev, nrow, ncol, chunks), name=...  200 us
    unnamed x10, local copies, waits for them, and re-layouts  5.31 us

profile of v1, /device:TPU:32, one launch (start us, length us, event | category | flops | bytes accessed | tf_op | source)
XLA Modules:
  0.0 206.2 jit_solution(15407497203675300446)
XLA Ops:
  0.6 0.0 copy-start
  0.6 1.6 copy-done
  2.2 0.0 copy-start.1
  2.2 0.8 copy-done.1
  3.1 0.0 copy-start.2
  3.1 0.8 copy-done.2
  3.8 0.0 copy-start.3
  3.8 0.7 copy-done.3
  4.5 200.2 %levels.1 = (bf16[128,128]{1,0:T(8,128)(2,1)S(1)}, bf16[128,128]{1,0:T(8,128)(2,1)S(1)}) custom-call(bf16[4,16,128,128]{3,2,1,0:T(8,128)(2,1)S(1)} %bitcast.12, s32[4,16]{1,0:T(4,128)S(1)} %bitcast.15, bf16[128,128]{1,0:T(8,128)(2,1)S(1)} %bitcast.14, f32[128,128]{1,0:T(8,128)S(1)} %bitcast.13), custom_call_target="tpu_custom_call" | custom-call | flops 1073741824 | bytes 4194304 | tf_op jit(solution)/shard_map/levels/pallas_call | solution.py:235
  204.7 0.7 copy.6
  205.4 0.7 copy.7
Async XLA Ops:
  0.6 1.6 copy-start
  2.2 0.8 copy-start.1
  3.1 0.8 copy-start.2
  3.8 0.7 copy-start.3

commit v2 on v1

v2 whole, which is shorter than its diff:
```python
import functools

import jax
import jax.numpy as jnp
from jax import lax
from jax.experimental import pallas as pl
from jax.experimental.pallas import tpu as pltpu
from jax.sharding import PartitionSpec as P

MESH = pl.DeviceIdType.MESH
BAND = 8
FAR_FIRST = sorted(range(-BAND, BAND + 1), key=lambda d: -abs(d))


def kernel(
    nlev, nrow, ncol, chunks,
    tiles_hbm, mask_hbm, inverse_hbm, sides_hbm,
    forward_ref, answer_ref,
    tiles_ref, mask_ref, inverse_ref, sides_ref,
    wf, wb, inv_t, sides_t,
    xin, part, part_f, yin, ysol, xsol, bin_, zout, zin, update,
    load_sem,
    fz_send, fz_recv, fy_send, fy_recv, by_send, by_recv, bz_send, bz_recv,
):
    l, z, c = lax.axis_index("level"), lax.axis_index("row"), lax.axis_index("col")
    rows = sides_ref.shape[0] // chunks
    side = sides_ref.shape[0]
    last = nlev - 1
    others = [lax.rem(c + o, ncol) for o in range(1, ncol)]

    loads = [
        pltpu.make_async_copy(src, dst, load_sem.at[n])
        for n, (src, dst) in enumerate((
            (sides_hbm, sides_ref), (inverse_hbm, inverse_ref),
            (mask_hbm, mask_ref), (tiles_hbm, tiles_ref)))
    ]
    for load in loads:
        load.start()

    def exists(d):
        return (z + d >= 0) & (z + d < nrow)

    for d in range(-BAND, BAND + 1):
        @pl.when(jnp.logical_not(exists(d)))
        def _():
            for k in range(chunks):
                xin[k, d + BAND] = jnp.zeros_like(xin[k, d + BAND])
                zin[k, d + BAND] = jnp.zeros_like(zin[k, d + BAND])

    barrier = pltpu.get_barrier_semaphore()
    for o in others:
        pl.semaphore_signal(barrier, inc=1, device_id=(l, z, o), device_id_type=MESH)

    @pl.when(l < last)
    def _():
        for q in range(nrow):
            pl.semaphore_signal(barrier, inc=1, device_id=(l + 1, q, c), device_id_type=MESH)

    @pl.when(l > 0)
    def _():
        for q in range(nrow):
            pl.semaphore_signal(barrier, inc=1, device_id=(l - 1, q, c), device_id_type=MESH)

    loads[0].wait()
    turned = sides_ref[...].T
    for k in range(chunks):
        sides_t[k] = turned[k * rows:(k + 1) * rows]
    loads[1].wait()
    inv_t[...] = inverse_ref[...].T
    update[...] = jnp.zeros_like(update)
    loads[2].wait()
    loads[3].wait()

    @pl.when(l > 0)
    def _():
        def prepare(slot, carry):
            q = z + slot - BAND
            at = pl.ds(pl.multiple_of(slot * side, side), side)

            @pl.when((q >= 0) & (q < nrow))
            def _():
                for a in range(ncol):
                    present = mask_ref[a, q].astype(jnp.float32)
                    tile = tiles_ref[a, q] * present.astype(jnp.bfloat16)
                    wb[slot, a * side:(a + 1) * side, :] = tile
                    wf[at, a * side:(a + 1) * side] = tile.T

            @pl.when((q < 0) | (q >= nrow))
            def _():
                wf[at, :] = jnp.zeros((side, ncol * side), wf.dtype)
            return carry
        lax.fori_loop(0, 2 * BAND + 1, prepare, 0)

    pl.semaphore_wait(
        barrier,
        (ncol - 1) + jnp.where(l > 0, nrow, 0) + jnp.where(l < last, nrow, 0),
    )

    def forward_copy(k, d):
        return pltpu.make_async_remote_copy(
            ysol.at[k], xin.at[k, BAND - d], fz_send.at[k, BAND + d], fz_recv.at[k, BAND - d],
            device_id=(l + 1, z + d, c), device_id_type=MESH)

    def backward_copy(k, d):
        return pltpu.make_async_remote_copy(
            zout.at[k, BAND + d], zin.at[k, BAND - d], bz_send.at[k, BAND + d], bz_recv.at[k, BAND - d],
            device_id=(l - 1, z + d, c), device_id_type=MESH)

    def part_copy(k, o):
        return pltpu.make_async_remote_copy(
            part.at[k, o], yin.at[k, c], fy_send.at[k, o], fy_recv.at[k, c],
            device_id=(l, z, o), device_id_type=MESH)

    def answer_copy(k, o):
        return pltpu.make_async_remote_copy(
            xsol.at[k], bin_.at[k, c], by_send.at[k, o], by_recv.at[k, c],
            device_id=(l, z, o), device_id_type=MESH)

    def arrived(dst, sem):
        pltpu.make_async_copy(dst, dst, sem).wait()

    def gather(buffer, sems, k, distances):
        for d in sorted(distances, key=abs):
            @pl.when(exists(d))
            def _():
                arrived(buffer.at[k, d + BAND], sems.at[k, d + BAND])

    near = range(-BAND + 2, BAND - 1)
    far_low, far_high = range(-BAND, -BAND + 2), range(BAND - 1, BAND + 1)
    far = [*far_low, *far_high]

    def product(k, distances):
        wide = jnp.concatenate([xin[k, d + BAND] for d in distances], axis=1)
        first = (distances[0] + BAND) * side
        return jnp.dot(
            wide, wf[first:first + len(distances) * side, :], preferred_element_type=jnp.float32)

    def forward_parts(k):
        gather(xin, fz_recv, k, near)
        total = product(k, near)
        gather(xin, fz_recv, k, far)
        total = total + (product(k, far_low) + product(k, far_high))
        for a in range(ncol):
            piece = total[:, a * side:(a + 1) * side]
            part_f[k, a] = piece
            part[k, a] = piece.astype(jnp.bfloat16)
        for o in others:
            part_copy(k, o).start()

    def forward_solve(k):
        @pl.when(l > 0)
        def _():
            mine = part_f[k, c]
            for o in others:
                arrived(yin.at[k, o], fy_recv.at[k, o])
                mine = mine + yin[k, o].astype(jnp.float32)
            update[...] = mine

        values = (sides_t[k] - update[...]).astype(jnp.bfloat16)
        ysol[k] = jnp.dot(
            values, inv_t[...], preferred_element_type=jnp.float32).astype(jnp.bfloat16)

        @pl.when(l < last)
        def _():
            for d in FAR_FIRST:
                @pl.when(exists(d))
                def _():
                    forward_copy(k, d).start()

    def backward_solve(k):
        def add(total, distances):
            return functools.reduce(
                jnp.add, [zin[k, d + BAND].astype(jnp.float32) for d in distances], total)

        @pl.when(l < last)
        def _():
            gather(zin, bz_recv, k, near)
            total = add(jnp.zeros_like(update), near)
            gather(zin, bz_recv, k, far)
            update[...] = add(total, far)

        @pl.when(l == last)
        def _():
            update[...] = jnp.zeros_like(update)

        values = (ysol[k].astype(jnp.float32) - update[...]).astype(jnp.bfloat16)
        xsol[k] = jnp.dot(
            values, inverse_ref[...], preferred_element_type=jnp.float32).astype(jnp.bfloat16)

        @pl.when(l > 0)
        def _():
            for o in others:
                answer_copy(k, o).start()
            bin_[k, c] = xsol[k]

    def backward_parts(k):
        for o in others:
            arrived(bin_.at[k, o], by_recv.at[k, o])
        wide = jnp.concatenate([bin_[k, a] for a in range(ncol)], axis=1)
        for d in FAR_FIRST:
            @pl.when(exists(d))
            def _():
                zout[k, d + BAND] = jnp.dot(
                    wide, wb[d + BAND], preferred_element_type=jnp.float32
                ).astype(jnp.bfloat16)
                backward_copy(k, d).start()

    def forward_sent(k):
        @pl.when(l > 0)
        def _():
            for o in others:
                part_copy(k, o).wait_send()

        @pl.when(l < last)
        def _():
            for d in FAR_FIRST:
                @pl.when(exists(d))
                def _():
                    forward_copy(k, d).wait_send()

    def backward_sent(k):
        @pl.when(l > 0)
        def _():
            for o in others:
                answer_copy(k, o).wait_send()
            for d in FAR_FIRST:
                @pl.when(exists(d))
                def _():
                    backward_copy(k, d).wait_send()

    at_last = l == last
    turn = jnp.where(at_last, 1, chunks + 1)

    def step(t, carry):
        def stage(k, wanted, work):
            @pl.when((k >= 0) & (k < chunks) & wanted)
            def _():
                work(k)

        stage(t, l > 0, forward_parts)
        stage(t - 1, True, forward_solve)
        stage(t - turn, True, backward_solve)
        stage(t - turn - 1, l > 0, backward_parts)
        stage(t - chunks - 1, True, forward_sent)
        return carry

    lax.fori_loop(0, 2 * chunks + 2, step, 0)
    lax.fori_loop(0, chunks, lambda j, x: (backward_sent(j), x)[1], 0)
    for k in range(chunks):
        forward_ref[k * rows:(k + 1) * rows] = ysol[k]
        answer_ref[k * rows:(k + 1) * rows] = xsol[k]


def local(factor_tiles, tile_mask, inverse_diagonal, right_sides):
    nlev, nrow, ncol = (lax.axis_size(n) for n in ("level", "row", "col"))
    tiles = factor_tiles[0, :, :, 0]
    mask = tile_mask[0, :, :, 0]
    inverse = inverse_diagonal[0, 0, 0]
    sides = right_sides[0, 0, 0]
    side, width = sides.shape
    chunks = 4
    rows = width // chunks
    bf16, f32 = jnp.bfloat16, jnp.float32
    vmem = pl.BlockSpec(memory_space=pltpu.VMEM)
    hbm = pl.BlockSpec(memory_space=pltpu.HBM)
    dma = pltpu.SemaphoreType.DMA
    slots = 2 * BAND + 1
    forward, answer = pl.pallas_call(
        functools.partial(kernel, nlev, nrow, ncol, chunks),
        name="levels",
        out_shape=[jax.ShapeDtypeStruct((width, side), bf16)] * 2,
        in_specs=[hbm] * 4,
        out_specs=[vmem, vmem],
        scratch_shapes=[
            pltpu.VMEM(tiles.shape, bf16),
            pltpu.SMEM(mask.shape, mask.dtype),
            pltpu.VMEM(inverse.shape, bf16),
            pltpu.VMEM(sides.shape, f32),
            pltpu.VMEM((slots * side, ncol * side), bf16),
            pltpu.VMEM((slots, ncol * side, side), bf16),
            pltpu.VMEM((side, side), bf16),
            pltpu.VMEM((chunks, rows, side), f32),
            pltpu.VMEM((chunks, slots, rows, side), bf16),
            pltpu.VMEM((chunks, ncol, rows, side), bf16),
            pltpu.VMEM((chunks, ncol, rows, side), f32),
            pltpu.VMEM((chunks, ncol, rows, side), bf16),
            pltpu.VMEM((chunks, rows, side), bf16),
            pltpu.VMEM((chunks, rows, side), bf16),
            pltpu.VMEM((chunks, ncol, rows, side), bf16),
            pltpu.VMEM((chunks, slots, rows, side), bf16),
            pltpu.VMEM((chunks, slots, rows, side), bf16),
            pltpu.VMEM((rows, side), f32),
            dma((4,)),
            dma((chunks, slots)), dma((chunks, slots)),
            dma((chunks, ncol)), dma((chunks, ncol)),
            dma((chunks, ncol)), dma((chunks, ncol)),
            dma((chunks, slots)), dma((chunks, slots)),
        ],
        compiler_params=pltpu.CompilerParams(
            collective_id=0, has_side_effects=True, vmem_limit_bytes=60 * 2**20),
        cost_estimate=pl.CostEstimate(flops=2**30, bytes_accessed=2**22, transcendentals=0),
    )(tiles, mask, inverse, sides)
    return (forward.T[None, None, None], answer.T[None, None, None])


def solution(mesh):
    placed = (
        P("level", "row", None, "col", None, None),
        P("level", "row", None, "col"),
        P("level", "row", "col", None, None),
        P("level", "row", "col", None, None),
    )
    return jax.shard_map(
        local,
        mesh=mesh,
        in_specs=placed,
        out_specs=(P("level", "row", "col", None, None), P("level", "row", "col", None, None)),
        check_vma=False,
    )
```

time: 206 us -> 193 us (0.937)
  the two profiles are of different devices: /device:TPU:32 before, /device:TPU:8 now
where the time goes in v2:
time: 193 us; the launch traced here: 192 us
  Pallas kernels  189 us (98%)
  local copies, waits for them, and re-layouts  2.95 us (2%)
    pallas_call x1, Pallas kernels, local(): pl.pallas_call(functools.partial(kernel, nlev, nrow, ncol, chunks), name=...  189 us

profile of v2, /device:TPU:8, one launch (start us, length us, event | category | flops | bytes accessed | tf_op | source)
XLA Modules:
  0.0 192.2 jit_solution(5841718160214198828)
XLA Ops:
  0.6 188.7 %levels.1 = (bf16[128,128]{1,0:T(8,128)(2,1)}, bf16[128,128]{1,0:T(8,128)(2,1)}) custom-call(bf16[4,16,128,128]{3,2,1,0:T(8,128)(2,1)} %bitcast.12, s32[4,16]{1,0:T(4,128)} %bitcast.15, bf16[128,128]{1,0:T(8,128)(2,1)} %bitcast.14, f32[128,128]{1,0:T(8,128)} %bitcast.13), custom_call_target="tpu_custom_call" | custom-call | flops 1073741824 | bytes 4194304 | tf_op jit(solution)/shard_map/levels/pallas_call | solution.py:268
  189.3 1.5 copy.6
  190.8 1.5 copy.7

commit v3 on v2

v3 whole, which is shorter than its diff:
```python
import functools

import jax
import jax.numpy as jnp
from jax import lax
from jax.experimental import pallas as pl
from jax.experimental.pallas import tpu as pltpu
from jax.sharding import PartitionSpec as P

MESH = pl.DeviceIdType.MESH
BAND = 8
SLOTS = 2 * BAND + 1
HALF = BAND + 1


def kernel(
    nlev, nrow, ncol, chunks, whole_from, early_from,
    tiles_hbm, mask_hbm, inverse_hbm, sides_hbm,
    forward_ref, answer_ref,
    tiles_ref, mask_ref, inverse_ref, sides_ref,
    wf, wb, inv, inv_t, sides_row, sides_use,
    xin, part, part_f, yin, ysol, zout, zin, update,
    ystage, ysplit, yblock, yturned, xstage, xblock, xturned,
    load_sem, fz_send, fz_recv, fy_send, fy_recv, bz_send, bz_recv,
    bulk_send, bulk_recv, d_send, d_recv, s_send, s_recv, y_send, y_recv, x_send, x_recv,
):
    l, z, c = lax.axis_index("level"), lax.axis_index("row"), lax.axis_index("col")
    side, width = sides_ref.shape
    rows = width // chunks
    unit = rows // ncol
    last = nlev - 1
    bf16, f32 = jnp.bfloat16, jnp.float32
    others = [lax.rem(c + o, ncol) for o in range(1, ncol)]
    after, before = others[0], others[-1]
    split_from = whole_from - 1

    loads = [
        pltpu.make_async_copy(src, dst, load_sem.at[n])
        for n, (src, dst) in enumerate((
            (sides_hbm, sides_ref), (inverse_hbm, inverse_ref),
            (mask_hbm, mask_ref), (tiles_hbm, tiles_ref)))
    ]
    for load in loads:
        load.start()

    def exists(d):
        return (z + d >= 0) & (z + d < nrow)

    for d in range(-BAND, BAND + 1):
        @pl.when(jnp.logical_not(exists(d)))
        def _():
            for k in range(chunks):
                xin[k, d + BAND] = jnp.zeros_like(xin[k, d + BAND])
                zin[k, d + BAND] = jnp.zeros_like(zin[k, d + BAND])

    barrier = pltpu.get_barrier_semaphore()
    for o in others:
        pl.semaphore_signal(barrier, inc=1, device_id=(l, z, o), device_id_type=MESH)

    @pl.when(l < last)
    def _():
        for q in range(nrow):
            pl.semaphore_signal(barrier, inc=1, device_id=(l + 1, q, c), device_id_type=MESH)

    @pl.when(l > 0)
    def _():
        for q in range(nrow):
            pl.semaphore_signal(barrier, inc=1, device_id=(l - 1, q, c), device_id_type=MESH)

    loads[0].wait()
    turned = sides_ref[...].T
    for o in range(ncol):
        sides_row[o] = turned[o * rows:(o + 1) * rows]
    loads[1].wait()
    inv[c] = inverse_ref[...]
    inv_t[c] = inverse_ref[...].T
    update[...] = jnp.zeros_like(update)
    loads[2].wait()
    loads[3].wait()

    @pl.when(l > 0)
    def _():
        def prepare(slot, carry):
            q = z + slot - BAND

            @pl.when((q >= 0) & (q < nrow))
            def _():
                for a in range(ncol):
                    present = mask_ref[a, q].astype(f32)
                    tile = tiles_ref[a, q] * present.astype(bf16)
                    wb[slot, c, a * side:(a + 1) * side, :] = tile
                    wf[slot, :, a * side:(a + 1) * side] = tile.T

            @pl.when((q < 0) | (q >= nrow))
            def _():
                wb[slot, c] = jnp.zeros((ncol * side, side), bf16)
                wf[slot] = jnp.zeros((side, ncol * side), bf16)
            return carry
        lax.fori_loop(0, SLOTS, prepare, 0)

    pl.semaphore_wait(
        barrier,
        (ncol - 1) + jnp.where(l > 0, nrow, 0) + jnp.where(l < last, nrow, 0),
    )

    def remote(src, dst, send, recv, device):
        return pltpu.make_async_remote_copy(
            src, dst, send, recv, device_id=device, device_id_type=MESH)

    def arrived(dst, sem):
        pltpu.make_async_copy(dst, dst, sem).wait()

    def forward_copy(k, d):
        return remote(
            ysol.at[k], xin.at[k, BAND - d], fz_send.at[k, BAND + d], fz_recv.at[k, BAND - d],
            (l + 1, z + d, c))

    def backward_copy(k, d):
        return remote(
            zout.at[k, BAND + d], zin.at[k, BAND - d], bz_send.at[k, BAND + d],
            bz_recv.at[k, BAND - d], (l - 1, z + d, c))

    def part_copy(k, o):
        return remote(
            part.at[k, o], yin.at[k, c], fy_send.at[k, o], fy_recv.at[k, c], (l, z, o))

    def turn_copy(src, dst, send, recv, o):
        return remote(src.at[o], dst.at[c], send.at[o], recv.at[c], (l, z, o))

    def turn_start(src, dst, send, recv):
        for o in others:
            turn_copy(src, dst, send, recv, o).start()
        dst[c] = src[c]

    def turn_arrived(dst, recv):
        for o in others:
            arrived(dst.at[o], recv.at[o])

    def turn_sent(src, dst, send, recv):
        for o in others:
            turn_copy(src, dst, send, recv, o).wait_send()

    def inverse_copy(o):
        return remote(inv.at[c], inv.at[c], d_send.at[o], d_recv.at[c], (l, z, o))

    low, high = pl.ds(0, HALF), pl.ds(HALF, SLOTS - HALF)

    def bulk_copy(slots, owner, n, device):
        return remote(
            wb.at[slots, owner], wb.at[slots, owner], bulk_send.at[n], bulk_recv.at[n],
            (l, z, device))

    def bulk_own():
        return [
            bulk_copy(low, c, 0, after), bulk_copy(high, c, 3, before),
            bulk_copy(high, c, 1, after), bulk_copy(low, c, 2, before),
        ]

    def bulk_passed():
        return [bulk_copy(low, before, 4, after), bulk_copy(high, after, 5, before)]

    def spread_tiles():
        for copy in bulk_own():
            copy.start()
        to_after, to_before = bulk_passed()
        arrived(wb.at[low, before], bulk_recv.at[0])
        to_after.start()
        arrived(wb.at[high, after], bulk_recv.at[3])
        to_before.start()
        arrived(wb.at[high, before], bulk_recv.at[1])
        arrived(wb.at[low, after], bulk_recv.at[2])
        opposite = others[1]
        arrived(wb.at[low, opposite], bulk_recv.at[4])
        arrived(wb.at[high, opposite], bulk_recv.at[5])

    def await_slot(buffer, sems, k, d):
        @pl.when(exists(d))
        def _():
            arrived(buffer.at[k, d + BAND], sems.at[k, d + BAND])

    def stacked(block, k):
        at = pl.ds(pl.multiple_of(k * unit, unit), unit)
        return jnp.concatenate([block[o, at] for o in range(ncol)], axis=0)

    def put(block, k, values):
        at = pl.ds(pl.multiple_of(k * unit, unit), unit)
        for o in range(ncol):
            block[o, at] = values[o * unit:(o + 1) * unit]

    def to_lanes(values):
        return jnp.concatenate([values[o * unit:(o + 1) * unit] for o in range(ncol)], axis=1)

    def to_rows(values):
        return jnp.concatenate([values[:, o * side:(o + 1) * side] for o in range(ncol)], axis=0)

    def tiles_of(slot):
        return jnp.concatenate([wb[slot, o] for o in range(ncol)], axis=1)

    def send_forward(k):
        @pl.when(l < last)
        def _():
            def at_distance(n, carry):
                for d in (n - BAND, BAND - n):
                    @pl.when(exists(d))
                    def _():
                        forward_copy(k, d).start()
                return carry
            lax.fori_loop(0, BAND, at_distance, 0)
            forward_copy(k, 0).start()

    def forward_parts(k):
        def at_distance(n, total):
            await_slot(xin, fz_recv, k, -n)
            await_slot(xin, fz_recv, k, n)
            wide = jnp.concatenate([xin[k, BAND - n], xin[k, BAND + n]], axis=1)
            weights = jnp.concatenate([wf[BAND - n], wf[BAND + n]], axis=0)
            return total + jnp.dot(wide, weights, preferred_element_type=f32)

        await_slot(xin, fz_recv, k, 0)
        total = lax.fori_loop(
            1, BAND + 1, at_distance,
            jnp.dot(xin[k, BAND], wf[BAND], preferred_element_type=f32))

        @pl.when(l < split_from)
        def _():
            for o in range(ncol):
                part_f[k, o] = total[:, o * side:(o + 1) * side]

        @pl.when(l == split_from)
        def _():
            for o in range(ncol):
                part_f[k, o] = to_rows(total[o * unit:(o + 1) * unit])

        for o in range(ncol):
            part[k, o] = part_f[k, o].astype(bf16)
        for o in others:
            part_copy(k, o).start()

    def add_parts(k):
        mine = part_f[k, c]
        for o in others:
            arrived(yin.at[k, o], fy_recv.at[k, o])
            mine = mine + yin[k, o].astype(f32)
        update[...] = mine

    def forward_row(k):
        @pl.when(l > 0)
        def _():
            add_parts(k)

        values = (stacked(sides_use, k) - update[...]).astype(bf16)
        solved = jnp.dot(values, inv_t[c], preferred_element_type=f32).astype(bf16)
        ysol[k] = solved
        send_forward(k)
        put(ystage, k, solved.astype(f32))

    def forward_split(k):
        @pl.when(l == split_from)
        def _():
            add_parts(k)

        @pl.when(l > split_from)
        def _():
            def product(slot):
                wide = to_lanes(xin[k, slot].astype(f32)).astype(bf16)
                return lax.dot_general(
                    wide, tiles_of(slot), (((1,), (1,)), ((), ())), preferred_element_type=f32)

            def at_distance(n, total):
                await_slot(xin, fz_recv, k, -n)
                await_slot(xin, fz_recv, k, n)
                return total + (product(BAND - n) + product(BAND + n))

            await_slot(xin, fz_recv, k, 0)
            total = lax.fori_loop(1, BAND + 1, at_distance, product(BAND))
            update[...] = to_rows(total)

        values = stacked(sides_use, k) - update[...]
        solved = jnp.concatenate(
            [
                jnp.dot(values[o * unit:(o + 1) * unit].astype(bf16), inv_t[o],
                        preferred_element_type=f32)
                for o in range(ncol)
            ],
            axis=0,
        ).astype(bf16)
        ysol[k] = solved
        send_forward(k)
        put(ystage, k, solved.astype(f32))
        put(ysplit, k, solved.astype(f32))

    def backward_step(k):
        def add(total, distances):
            return functools.reduce(
                jnp.add, [zin[k, d + BAND].astype(f32) for d in distances], total)

        @pl.when(l < last)
        def _():
            near = sorted(range(-BAND + 1, BAND), key=abs)
            for d in near:
                await_slot(zin, bz_recv, k, d)
            total = add(jnp.zeros_like(update), near)
            await_slot(zin, bz_recv, k, -BAND)
            await_slot(zin, bz_recv, k, BAND)
            update[...] = add(total, (-BAND, BAND))

        @pl.when(l == last)
        def _():
            update[...] = jnp.zeros_like(update)

        values = stacked(ysplit, k) - update[...]
        wide = jnp.concatenate(
            [
                jnp.dot(values[o * unit:(o + 1) * unit].astype(bf16), inv[o],
                        preferred_element_type=f32)
                for o in range(ncol)
            ],
            axis=1,
        ).astype(bf16)

        @pl.when(l > 0)
        def _():
            def send(d):
                @pl.when(exists(d))
                def _():
                    zout[k, d + BAND] = to_rows(jnp.dot(
                        wide, tiles_of(d + BAND), preferred_element_type=f32)).astype(bf16)
                    backward_copy(k, d).start()

            def at_distance(n, carry):
                send(n - BAND)
                send(BAND - n)
                return carry
            lax.fori_loop(0, BAND, at_distance, 0)
            send(0)

        put(xstage, k, to_rows(wide.astype(f32)))

    def sent(copy_of):
        def one(k, carry):
            for d in range(-BAND, BAND + 1):
                @pl.when(exists(d))
                def _():
                    copy_of(k, d).wait_send()
            return carry
        lax.fori_loop(0, chunks, one, 0)

    def middle():
        yblock[...] = ystage[...].astype(bf16)
        turn_start(yblock, yturned, y_send, y_recv)

        @pl.when((l > 0) & (l < early_from))
        def _():
            spread_tiles()

        @pl.when(l < last)
        def _():
            sent(forward_copy)

        @pl.when((l > 0) & (l < whole_from))
        def _():
            def one(k, carry):
                for o in others:
                    part_copy(k, o).wait_send()
                return carry
            lax.fori_loop(0, chunks, one, 0)

        turn_arrived(yturned, y_recv)
        turn_sent(yblock, yturned, y_send, y_recv)

        @pl.when(l < split_from)
        def _():
            ysplit[...] = yturned[...].astype(f32)
            forward_ref[...] = yblock[...].reshape(width, side)

        @pl.when(l >= split_from)
        def _():
            forward_ref[...] = yturned[...].reshape(width, side)

    for o in others:
        inverse_copy(o).start()

    @pl.when(l < split_from)
    def _():
        sides_use[...] = sides_row[...]

    @pl.when(l >= split_from)
    def _():
        turn_start(sides_row, sides_use, s_send, s_recv)
        turn_arrived(sides_use, s_recv)
        for o in others:
            arrived(inv.at[o], d_recv.at[o])
            inv_t[o] = inv[o].T
        turn_sent(sides_row, sides_use, s_send, s_recv)

    @pl.when(l >= early_from)
    def _():
        spread_tiles()

    at_last = l == last
    turn = jnp.where(at_last, 1, chunks + 1)

    def step(t, carry):
        def stage(k, wanted, work):
            @pl.when((k >= 0) & (k < chunks) & wanted)
            def _():
                work(k)

        stage(t, (l > 0) & (l < whole_from), forward_parts)
        stage(t - 1, l < split_from, forward_row)
        stage(t - 1, l >= split_from, forward_split)
        stage(t - turn, True, backward_step)

        @pl.when(t == chunks)
        def _():
            @pl.when(l < split_from)
            def _():
                for o in others:
                    arrived(inv.at[o], d_recv.at[o])
            middle()
        return carry

    lax.fori_loop(0, 2 * chunks + 1, step, 0)

    xblock[...] = xstage[...].astype(bf16)
    turn_start(xblock, xturned, x_send, x_recv)
    for o in others:
        inverse_copy(o).wait_send()

    @pl.when(l > 0)
    def _():
        sent(backward_copy)
        for copy in (*bulk_own(), *bulk_passed()):
            copy.wait_send()
    turn_arrived(xturned, x_recv)
    answer_ref[...] = xturned[...].reshape(width, side)
    turn_sent(xblock, xturned, x_send, x_recv)


def local(factor_tiles, tile_mask, inverse_diagonal, right_sides):
    nlev, nrow, ncol = (lax.axis_size(n) for n in ("level", "row", "col"))
    tiles = factor_tiles[0, :, :, 0]
    mask = tile_mask[0, :, :, 0]
    inverse = inverse_diagonal[0, 0, 0]
    sides = right_sides[0, 0, 0]
    side, width = sides.shape
    chunks = 4
    rows = width // chunks
    bf16, f32 = jnp.bfloat16, jnp.float32
    vmem = pl.BlockSpec(memory_space=pltpu.VMEM)
    hbm = pl.BlockSpec(memory_space=pltpu.HBM)
    dma = pltpu.SemaphoreType.DMA
    blocks = (ncol, rows, side)
    forward, answer = pl.pallas_call(
        functools.partial(kernel, nlev, nrow, ncol, chunks, nlev - 3, nlev - 3),
        name="levels",
        out_shape=[jax.ShapeDtypeStruct((width, side), bf16)] * 2,
        in_specs=[hbm] * 4,
        out_specs=[vmem, vmem],
        scratch_shapes=[
            pltpu.VMEM(tiles.shape, bf16),
            pltpu.SMEM(mask.shape, mask.dtype),
            pltpu.VMEM(inverse.shape, bf16),
            pltpu.VMEM(sides.shape, f32),
            pltpu.VMEM((SLOTS, side, ncol * side), bf16),
            pltpu.VMEM((SLOTS, ncol, ncol * side, side), bf16),
            pltpu.VMEM((ncol, side, side), bf16),
            pltpu.VMEM((ncol, side, side), bf16),
            pltpu.VMEM(blocks, f32),
            pltpu.VMEM(blocks, f32),
            pltpu.VMEM((chunks, SLOTS, rows, side), bf16),
            pltpu.VMEM((chunks, *blocks), bf16),
            pltpu.VMEM((chunks, *blocks), f32),
            pltpu.VMEM((chunks, *blocks), bf16),
            pltpu.VMEM((chunks, rows, side), bf16),
            pltpu.VMEM((chunks, SLOTS, rows, side), bf16),
            pltpu.VMEM((chunks, SLOTS, rows, side), bf16),
            pltpu.VMEM((rows, side), f32),
            pltpu.VMEM(blocks, f32),
            pltpu.VMEM(blocks, f32),
            pltpu.VMEM(blocks, bf16),
            pltpu.VMEM(blocks, bf16),
            pltpu.VMEM(blocks, f32),
            pltpu.VMEM(blocks, bf16),
            pltpu.VMEM(blocks, bf16),
            dma((4,)),
            dma((chunks, SLOTS)), dma((chunks, SLOTS)),
            dma((chunks, ncol)), dma((chunks, ncol)),
            dma((chunks, SLOTS)), dma((chunks, SLOTS)),
            dma((6,)), dma((6,)),
            *[dma((ncol,)) for _ in range(8)],
        ],
        compiler_params=pltpu.CompilerParams(
            collective_id=0, has_side_effects=True, vmem_limit_bytes=60 * 2**20),
        cost_estimate=pl.CostEstimate(flops=2**30, bytes_accessed=2**22, transcendentals=0),
    )(tiles, mask, inverse, sides)
    return (forward.T[None, None, None], answer.T[None, None, None])


def solution(mesh):
    placed = (
        P("level", "row", None, "col", None, None),
        P("level", "row", None, "col"),
        P("level", "row", "col", None, None),
        P("level", "row", "col", None, None),
    )
    return jax.shard_map(
        local,
        mesh=mesh,
        in_specs=placed,
        out_specs=(P("level", "row", "col", None, None), P("level", "row", "col", None, None)),
        check_vma=False,
    )
```

time: 193 us -> 194 us (level)
  the two profiles are of different devices: /device:TPU:8 before, /device:TPU:32 now
where the time goes in v3:
time: 194 us; the launch traced here: 193 us
  Pallas kernels  190 us (98%)
  local copies, waits for them, and re-layouts  2.95 us (2%)
    pallas_call x1, Pallas kernels, local(): pl.pallas_call(functools.partial(kernel, nlev, nrow, ncol, chunks, nlev -...  190 us

profile of v3, /device:TPU:32, one launch (start us, length us, event | category | flops | bytes accessed | tf_op | source)
XLA Modules:
  0.0 193.4 jit_solution(13224423332644836348)
XLA Ops:
  0.6 189.8 %levels.1 = (bf16[128,128]{1,0:T(8,128)(2,1)}, bf16[128,128]{1,0:T(8,128)(2,1)}) custom-call(bf16[4,16,128,128]{3,2,1,0:T(8,128)(2,1)} %bitcast.12, s32[4,16]{1,0:T(4,128)} %bitcast.15, bf16[128,128]{1,0:T(8,128)(2,1)} %bitcast.14, f32[128,128]{1,0:T(8,128)} %bitcast.13), custom_call_target="tpu_custom_call" | custom-call | flops 1073741824 | bytes 4194304 | tf_op jit(solution)/shard_map/levels/pallas_call | solution.py:454
  190.5 1.5 copy.6
  192.0 1.5 copy.7

commit v4 on v3

--- a/solution.py
+++ b/solution.py
@@ -11,18 +11,21 @@
 BAND = 8
 SLOTS = 2 * BAND + 1
 HALF = BAND + 1
+FAR_FIRST = sorted(range(-BAND, BAND + 1), key=lambda d: -abs(d))
 
 
 def kernel(
-    nlev, nrow, ncol, chunks, whole_from, early_from,
+    nlev, nrow, ncol, chunks, whole_from,
     tiles_hbm, mask_hbm, inverse_hbm, sides_hbm,
     forward_ref, answer_ref,
     tiles_ref, mask_ref, inverse_ref, sides_ref,
-    wf, wb, inv, inv_t, sides_row, sides_use,
+    wt, wb, inv, inv_t, sides_row, sides_use,
     xin, part, part_f, yin, ysol, zout, zin, update,
     ystage, ysplit, yblock, yturned, xstage, xblock, xturned,
     load_sem, fz_send, fz_recv, fy_send, fy_recv, bz_send, bz_recv,
     bulk_send, bulk_recv, d_send, d_recv, s_send, s_recv, y_send, y_recv, x_send, x_recv,
+    sides_guest, inv_guest, inv_t_guest, ysplit_guest, xstage_guest, yblock_guest, xblock_guest,
+    ship_send, ship_recv, go_sem,
 ):
     l, z, c = lax.axis_index("level"), lax.axis_index("row"), lax.axis_index("col")
     side, width = sides_ref.shape
@@ -33,6 +36,7 @@
     others = [lax.rem(c + o, ncol) for o in range(1, ncol)]
     after, before = others[0], others[-1]
     split_from = whole_from - 1
+    up, down = lax.rem(l + 1, last), lax.rem(l + last - 1, last)
 
     loads = [
         pltpu.make_async_copy(src, dst, load_sem.at[n])
@@ -60,12 +64,16 @@
     @pl.when(l < last)
     def _():
         for q in range(nrow):
-            pl.semaphore_signal(barrier, inc=1, device_id=(l + 1, q, c), device_id_type=MESH)
-
-    @pl.when(l > 0)
-    def _():
-        for q in range(nrow):
-            pl.semaphore_signal(barrier, inc=1, device_id=(l - 1, q, c), device_id_type=MESH)
+            pl.semaphore_signal(barrier, inc=1, device_id=(up, q, c), device_id_type=MESH)
+            pl.semaphore_signal(barrier, inc=1, device_id=(down, q, c), device_id_type=MESH)
+
+    @pl.when(l == 0)
+    def _():
+        pl.semaphore_signal(barrier, inc=1, device_id=(last, z, c), device_id_type=MESH)
+
+    @pl.when(l == last)
+    def _():
+        pl.semaphore_signal(barrier, inc=1, device_id=(0, z, c), device_id_type=MESH)
 
     loads[0].wait()
     turned = sides_ref[...].T
@@ -89,18 +97,20 @@
                     present = mask_ref[a, q].astype(f32)
                     tile = tiles_ref[a, q] * present.astype(bf16)
                     wb[slot, c, a * side:(a + 1) * side, :] = tile
-                    wf[slot, :, a * side:(a + 1) * side] = tile.T
+                    wt[slot, c, :, a * side:(a + 1) * side] = tile.T
 
             @pl.when((q < 0) | (q >= nrow))
             def _():
                 wb[slot, c] = jnp.zeros((ncol * side, side), bf16)
-                wf[slot] = jnp.zeros((side, ncol * side), bf16)
+                wt[slot, c] = jnp.zeros((side, ncol * side), bf16)
             return carry
         lax.fori_loop(0, SLOTS, prepare, 0)
 
     pl.semaphore_wait(
         barrier,
-        (ncol - 1) + jnp.where(l > 0, nrow, 0) + jnp.where(l < last, nrow, 0),
+        (ncol - 1)
+        + jnp.where(l < last, 2 * nrow, 1)
+        + jnp.where(l == 0, 1, 0),
     )
 
     def remote(src, dst, send, recv, device):
@@ -113,12 +123,12 @@
     def forward_copy(k, d):
         return remote(
             ysol.at[k], xin.at[k, BAND - d], fz_send.at[k, BAND + d], fz_recv.at[k, BAND - d],
-            (l + 1, z + d, c))
+            (up, z + d, c))
 
     def backward_copy(k, d):
         return remote(
             zout.at[k, BAND + d], zin.at[k, BAND - d], bz_send.at[k, BAND + d],
-            bz_recv.at[k, BAND - d], (l - 1, z + d, c))
+            bz_recv.at[k, BAND - d], (down, z + d, c))
 
     def part_copy(k, o):
         return remote(
@@ -159,9 +169,23 @@
     def bulk_passed():
         return [bulk_copy(low, before, 4, after), bulk_copy(high, after, 5, before)]
 
-    def spread_tiles():
+    opposite = others[1]
+
+    def transpose_tiles(owner):
+        @pl.when((l >= whole_from) | (l == 0))
+        def _():
+            def one(slot, carry):
+                for a in range(ncol):
+                    at = slice(a * side, (a + 1) * side)
+                    wt[slot, owner, :, at] = wb[slot, owner, at, :].T
+                return carry
+            lax.fori_loop(0, SLOTS, one, 0)
+
+    def spread_start():
         for copy in bulk_own():
             copy.start()
+
+    def spread_pass_on():
         to_after, to_before = bulk_passed()
         arrived(wb.at[low, before], bulk_recv.at[0])
         to_after.start()
@@ -169,9 +193,32 @@
         to_before.start()
         arrived(wb.at[high, before], bulk_recv.at[1])
         arrived(wb.at[low, after], bulk_recv.at[2])
-        opposite = others[1]
+
+    def spread_end():
+        transpose_tiles(before)
+        transpose_tiles(after)
         arrived(wb.at[low, opposite], bulk_recv.at[4])
         arrived(wb.at[high, opposite], bulk_recv.at[5])
+        transpose_tiles(opposite)
+
+    def ship(n, src, dst, device):
+        return remote(src, dst, ship_send.at[n], ship_recv.at[n], (device, z, c))
+
+    def ship_out():
+        return [
+            ship(1, sides_use, sides_guest, 0), ship(2, inv, inv_guest, 0),
+            ship(3, inv_t, inv_t_guest, 0),
+            ship(0, wb.at[:, c], wb.at[:, c], 0),
+        ]
+
+    def ship_back_y():
+        return ship(4, yblock_guest, yblock, last)
+
+    def ship_back_x():
+        return ship(5, xblock_guest, xblock, last)
+
+    def go(device):
+        pl.semaphore_signal(go_sem, inc=1, device_id=(device, z, c), device_id_type=MESH)
 
     def await_slot(buffer, sems, k, d):
         @pl.when(exists(d))
@@ -197,29 +244,29 @@
         return jnp.concatenate([wb[slot, o] for o in range(ncol)], axis=1)
 
     def send_forward(k):
-        @pl.when(l < last)
-        def _():
-            def at_distance(n, carry):
-                for d in (n - BAND, BAND - n):
-                    @pl.when(exists(d))
-                    def _():
-                        forward_copy(k, d).start()
-                return carry
-            lax.fori_loop(0, BAND, at_distance, 0)
-            forward_copy(k, 0).start()
+        for d in FAR_FIRST:
+            @pl.when(exists(d))
+            def _():
+                forward_copy(k, d).start()
+
+    near = range(-BAND + 3, BAND - 2)
+    middling = [-BAND + 2, BAND - 2, -BAND + 1, BAND - 1]
+    far = [-BAND, BAND]
+
+    def await_slots(buffer, sems, k, distances):
+        for d in sorted(distances, key=abs):
+            await_slot(buffer, sems, k, d)
 
     def forward_parts(k):
-        def at_distance(n, total):
-            await_slot(xin, fz_recv, k, -n)
-            await_slot(xin, fz_recv, k, n)
-            wide = jnp.concatenate([xin[k, BAND - n], xin[k, BAND + n]], axis=1)
-            weights = jnp.concatenate([wf[BAND - n], wf[BAND + n]], axis=0)
-            return total + jnp.dot(wide, weights, preferred_element_type=f32)
-
-        await_slot(xin, fz_recv, k, 0)
-        total = lax.fori_loop(
-            1, BAND + 1, at_distance,
-            jnp.dot(xin[k, BAND], wf[BAND], preferred_element_type=f32))
+        def product(distances):
+            wide = jnp.concatenate([xin[k, d + BAND] for d in distances], axis=1)
+            weights = jnp.concatenate([wt[d + BAND, c] for d in distances], axis=0)
+            return jnp.dot(wide, weights, preferred_element_type=f32)
+
+        total = 0.0
+        for distances in (near, middling, far):
+            await_slots(xin, fz_recv, k, distances)
+            total = total + product(distances)
 
         @pl.when(l < split_from)
         def _():
@@ -254,87 +301,81 @@
         send_forward(k)
         put(ystage, k, solved.astype(f32))
 
-    def forward_split(k):
-        @pl.when(l == split_from)
-        def _():
-            add_parts(k)
-
-        @pl.when(l > split_from)
-        def _():
-            def product(slot):
-                wide = to_lanes(xin[k, slot].astype(f32)).astype(bf16)
-                return lax.dot_general(
-                    wide, tiles_of(slot), (((1,), (1,)), ((), ())), preferred_element_type=f32)
-
-            def at_distance(n, total):
-                await_slot(xin, fz_recv, k, -n)
-                await_slot(xin, fz_recv, k, n)
-                return total + (product(BAND - n) + product(BAND + n))
-
-            await_slot(xin, fz_recv, k, 0)
-            total = lax.fori_loop(1, BAND + 1, at_distance, product(BAND))
-            update[...] = to_rows(total)
-
-        values = stacked(sides_use, k) - update[...]
-        solved = jnp.concatenate(
+    def whole_product(k):
+        def product(distances):
+            return functools.reduce(jnp.add, [
+                jnp.dot(
+                    to_lanes(xin[k, d + BAND].astype(f32)).astype(bf16),
+                    wt[d + BAND].reshape(ncol * side, ncol * side),
+                    preferred_element_type=f32)
+                for d in distances
+            ])
+
+        total = 0.0
+        for distances in (near, middling, far):
+            await_slots(xin, fz_recv, k, distances)
+            total = total + product(distances)
+        return to_rows(total)
+
+    def solve_split(values, blocks, axis):
+        return jnp.concatenate(
             [
-                jnp.dot(values[o * unit:(o + 1) * unit].astype(bf16), inv_t[o],
+                jnp.dot(values[o * unit:(o + 1) * unit].astype(bf16), blocks[o],
                         preferred_element_type=f32)
                 for o in range(ncol)
             ],
-            axis=0,
+            axis=axis,
         ).astype(bf16)
+
+    def forward_split(k):
+        @pl.when(l == split_from)
+        def _():
+            add_parts(k)
+
+        @pl.when(l > split_from)
+        def _():
+            update[...] = whole_product(k)
+
+        solved = solve_split(stacked(sides_use, k) - update[...], inv_t, 0)
         ysol[k] = solved
         send_forward(k)
         put(ystage, k, solved.astype(f32))
         put(ysplit, k, solved.astype(f32))
 
+    def backward_parts(k, wide):
+        for distances in (far, middling, sorted(near, key=lambda d: -abs(d))):
+            for d in distances:
+                zout[k, d + BAND] = to_rows(jnp.dot(
+                    wide, tiles_of(d + BAND), preferred_element_type=f32)).astype(bf16)
+            for d in distances:
+                @pl.when(exists(d))
+                def _():
+                    backward_copy(k, d).start()
+
     def backward_step(k):
         def add(total, distances):
             return functools.reduce(
                 jnp.add, [zin[k, d + BAND].astype(f32) for d in distances], total)
 
-        @pl.when(l < last)
-        def _():
-            near = sorted(range(-BAND + 1, BAND), key=abs)
-            for d in near:
-                await_slot(zin, bz_recv, k, d)
-            total = add(jnp.zeros_like(update), near)
-            await_slot(zin, bz_recv, k, -BAND)
-            await_slot(zin, bz_recv, k, BAND)
-            update[...] = add(total, (-BAND, BAND))
-
-        @pl.when(l == last)
-        def _():
-            update[...] = jnp.zeros_like(update)
-
-        values = stacked(ysplit, k) - update[...]
-        wide = jnp.concatenate(
-            [
-                jnp.dot(values[o * unit:(o + 1) * unit].astype(bf16), inv[o],
-                        preferred_element_type=f32)
-                for o in range(ncol)
-            ],
-            axis=1,
-        ).astype(bf16)
+        total = jnp.zeros_like(update)
+        for distances in ([*near, *middling], far):
+            await_slots(zin, bz_recv, k, distances)
+            total = add(total, distances)
+        wide = solve_split(stacked(ysplit, k) - total, inv, 1)
 
         @pl.when(l > 0)
         def _():
-            def send(d):
-                @pl.when(exists(d))
-                def _():
-                    zout[k, d + BAND] = to_rows(jnp.dot(
-                        wide, tiles_of(d + BAND), preferred_element_type=f32)).astype(bf16)
-                    backward_copy(k, d).start()
-
-            def at_distance(n, carry):
-                send(n - BAND)
-                send(BAND - n)
-                return carry
-            lax.fori_loop(0, BAND, at_distance, 0)
-            send(0)
+            backward_parts(k, wide)
 
         put(xstage, k, to_rows(wide.astype(f32)))
+
+    def guest_step(k, carry):
+        solved = solve_split(stacked(sides_guest, k) - whole_product(k), inv_t_guest, 0)
+        put(ysplit_guest, k, solved.astype(f32))
+        wide = solve_split(solved.astype(f32), inv_guest, 1)
+        backward_parts(k, wide)
+        put(xstage_guest, k, to_rows(wide.astype(f32)))
+        return carry
 
     def sent(copy_of):
         def one(k, carry):
@@ -346,12 +387,30 @@
         lax.fori_loop(0, chunks, one, 0)
 
     def middle():
-        yblock[...] = ystage[...].astype(bf16)
+        @pl.when(l < last)
+        def _():
+            yblock[...] = ystage[...].astype(bf16)
+
+        @pl.when(l == last)
+        def _():
+            arrived(yblock, ship_recv.at[4])
+
         turn_start(yblock, yturned, y_send, y_recv)
 
-        @pl.when((l > 0) & (l < early_from))
-        def _():
-            spread_tiles()
+        @pl.when((l == 1) | (l == 2))
+        def _():
+            pl.semaphore_wait(go_sem, 1)
+
+        @pl.when((l == 1) | (l == 2) | (l == 4))
+        def _():
+            spread_start()
+            spread_pass_on()
+            spread_end()
+
+        @pl.when(l == 3)
+        def _():
+            go(2)
+            spread_end()
 
         @pl.when(l < last)
         def _():
@@ -370,12 +429,33 @@
 
         @pl.when(l < split_from)
         def _():
+            for o in others:
+                arrived(inv.at[o], d_recv.at[o])
             ysplit[...] = yturned[...].astype(f32)
             forward_ref[...] = yblock[...].reshape(width, side)
 
         @pl.when(l >= split_from)
         def _():
             forward_ref[...] = yturned[...].reshape(width, side)
+
+    def guest():
+        arrived(wb.at[:, c], ship_recv.at[0])
+        spread_start()
+        transpose_tiles(c)
+        spread_pass_on()
+        spread_end()
+        go(1)
+        arrived(sides_guest, ship_recv.at[1])
+        arrived(inv_guest, ship_recv.at[2])
+        arrived(inv_t_guest, ship_recv.at[3])
+        lax.fori_loop(0, chunks, guest_step, 0)
+        yblock_guest[...] = ysplit_guest[...].astype(bf16)
+        ship_back_y().start()
+        xblock_guest[...] = xstage_guest[...].astype(bf16)
+        ship_back_x().start()
+        sent(backward_copy)
+        ship_back_y().wait_send()
+        ship_back_x().wait_send()
 
     for o in others:
         inverse_copy(o).start()
@@ -393,48 +473,76 @@
             inv_t[o] = inv[o].T
         turn_sent(sides_row, sides_use, s_send, s_recv)
 
-    @pl.when(l >= early_from)
-    def _():
-        spread_tiles()
-
-    at_last = l == last
-    turn = jnp.where(at_last, 1, chunks + 1)
-
-    def step(t, carry):
-        def stage(k, wanted, work):
-            @pl.when((k >= 0) & (k < chunks) & wanted)
-            def _():
-                work(k)
-
-        stage(t, (l > 0) & (l < whole_from), forward_parts)
-        stage(t - 1, l < split_from, forward_row)
-        stage(t - 1, l >= split_from, forward_split)
-        stage(t - turn, True, backward_step)
-
-        @pl.when(t == chunks)
-        def _():
-            @pl.when(l < split_from)
-            def _():
-                for o in others:
-                    arrived(inv.at[o], d_recv.at[o])
-            middle()
-        return carry
-
-    lax.fori_loop(0, 2 * chunks + 1, step, 0)
-
-    xblock[...] = xstage[...].astype(bf16)
+    @pl.when(l == last)
+    def _():
+        for copy in ship_out():
+            copy.start()
+
+    @pl.when((l == 3) | ((l >= 5) & (l < last)))
+    def _():
+        spread_start()
+        spread_pass_on()
+
+    @pl.when((l >= 5) & (l < last))
+    def _():
+        spread_end()
+
+    @pl.when(l < last)
+    def _():
+        def step(t, carry):
+            def stage(k, wanted, work):
+                @pl.when((k >= 0) & (k < chunks) & wanted)
+                def _():
+                    work(k)
+
+            stage(t, (l > 0) & (l < whole_from), forward_parts)
+            stage(t - 1, l < split_from, forward_row)
+            stage(t - 1, l >= split_from, forward_split)
+            return carry
+
+        lax.fori_loop(0, chunks + 1, step, 0)
+
+    middle()
+
+    @pl.when(l == 0)
+    def _():
+        guest()
+
+    @pl.when(l < last)
+    def _():
+        lax.fori_loop(0, chunks, lambda k, x: (backward_step(k), x)[1], 0)
+        xblock[...] = xstage[...].astype(bf16)
+
+    @pl.when(l == last)
+    def _():
+        arrived(xblock, ship_recv.at[5])
+
     turn_start(xblock, xturned, x_send, x_recv)
     for o in others:
         inverse_copy(o).wait_send()
 
-    @pl.when(l > 0)
+    @pl.when((l > 0) & (l < last))
     def _():
         sent(backward_copy)
+
+    @pl.when(l < last)
+    def _():
         for copy in (*bulk_own(), *bulk_passed()):
             copy.wait_send()
+
+    @pl.when(l == last)
+    def _():
+        for copy in ship_out():
+            copy.wait_send()
+
     turn_arrived(xturned, x_recv)
     answer_ref[...] = xturned[...].reshape(width, side)
     turn_sent(xblock, xturned, x_send, x_recv)
+
+
+def upright(forward_ref, answer_ref, forward_out, answer_out):
+    forward_out[...] = forward_ref[...].T
+    answer_out[...] = answer_ref[...].T
 
 
 def local(factor_tiles, tile_mask, inverse_diagonal, right_sides):
@@ -452,7 +560,7 @@
     dma = pltpu.SemaphoreType.DMA
     blocks = (ncol, rows, side)
     forward, answer = pl.pallas_call(
-        functools.partial(kernel, nlev, nrow, ncol, chunks, nlev - 3, nlev - 3),
+        functools.partial(kernel, nlev, nrow, ncol, chunks, nlev - 3),
         name="levels",
         out_shape=[jax.ShapeDtypeStruct((width, side), bf16)] * 2,
         in_specs=[hbm] * 4,
@@ -462,7 +570,7 @@
             pltpu.SMEM(mask.shape, mask.dtype),
             pltpu.VMEM(inverse.shape, bf16),
             pltpu.VMEM(sides.shape, f32),
-            pltpu.VMEM((SLOTS, side, ncol * side), bf16),
+            pltpu.VMEM((SLOTS, ncol, side, ncol * side), bf16),
             pltpu.VMEM((SLOTS, ncol, ncol * side, side), bf16),
             pltpu.VMEM((ncol, side, side), bf16),
             pltpu.VMEM((ncol, side, side), bf16),
@@ -489,12 +597,28 @@
             dma((chunks, SLOTS)), dma((chunks, SLOTS)),
             dma((6,)), dma((6,)),
             *[dma((ncol,)) for _ in range(8)],
+            pltpu.VMEM(blocks, f32),
+            pltpu.VMEM((ncol, side, side), bf16),
+            pltpu.VMEM((ncol, side, side), bf16),
+            pltpu.VMEM(blocks, f32),
+            pltpu.VMEM(blocks, f32),
+            pltpu.VMEM(blocks, bf16),
+            pltpu.VMEM(blocks, bf16),
+            dma((6,)), dma((6,)),
+            pltpu.SemaphoreType.REGULAR,
         ],
         compiler_params=pltpu.CompilerParams(
             collective_id=0, has_side_effects=True, vmem_limit_bytes=60 * 2**20),
         cost_estimate=pl.CostEstimate(flops=2**30, bytes_accessed=2**22, transcendentals=0),
     )(tiles, mask, inverse, sides)
-    return (forward.T[None, None, None], answer.T[None, None, None])
+    forward, answer = pl.pallas_call(
+        upright,
+        name="upright",
+        out_shape=[jax.ShapeDtypeStruct((side, width), bf16)] * 2,
+        in_specs=[vmem, vmem],
+        out_specs=[vmem, vmem],
+    )(forward, answer)
+    return (forward[None, None, None], answer[None, None, None])
 
 
 def solution(mesh):

time: 194 us -> 181 us (0.933)
  Pallas kernels: 190 us -> 180 us
  local copies, waits for them, and re-layouts: 2.95 us -> 0 us
    pallas_call x1, Pallas kernels: 190 us -> 179 us  [local(): pl.pallas_call(functools.partial(kernel, nlev, nrow, ncol, chunks, nlev -...]
    unnamed x2 -> x0, local copies, waits for them, and re-layouts: 2.95 us -> none
where the time goes in v4:
time: 181 us
  Pallas kernels  180 us (99%)
    pallas_call x1, Pallas kernels, local(): pl.pallas_call(functools.partial(kernel, nlev, nrow, ncol, chunks, nlev -...  179 us

profile of v4, /device:TPU:32, one launch (start us, length us, event | category | flops | bytes accessed | tf_op | source)
XLA Modules:
  0.0 180.7 jit_solution(196974268794271014)
XLA Ops:
  0.6 178.6 %levels.1 = (bf16[128,128]{1,0:T(8,128)(2,1)}, bf16[128,128]{1,0:T(8,128)(2,1)}) custom-call(bf16[4,16,128,128]{3,2,1,0:T(8,128)(2,1)} %bitcast.6, s32[4,16]{1,0:T(4,128)} %bitcast.11, bf16[128,128]{1,0:T(8,128)(2,1)} %bitcast.8, f32[128,128]{1,0:T(8,128)} %bitcast.7), custom_call_target="tpu_custom_call" | custom-call | flops 1073741824 | bytes 4194304 | tf_op jit(solution)/shard_map/levels/pallas_call | solution.py:562
  179.3 1.5 upright.1

commit v5 on v4

--- a/solution.py
+++ b/solution.py
@@ -24,10 +24,16 @@
     ystage, ysplit, yblock, yturned, xstage, xblock, xturned,
     load_sem, fz_send, fz_recv, fy_send, fy_recv, bz_send, bz_recv,
     bulk_send, bulk_recv, d_send, d_recv, s_send, s_recv, y_send, y_recv, x_send, x_recv,
-    sides_guest, inv_guest, inv_t_guest, ysplit_guest, xstage_guest, yblock_guest, xblock_guest,
-    ship_send, ship_recv, go_sem,
+    home_wb, home_sides, yfinal, xfinal, yhome, xhome,
+    ship_send, ship_recv, go_sem, near_total,
 ):
-    l, z, c = lax.axis_index("level"), lax.axis_index("row"), lax.axis_index("col")
+    p, z, c = lax.axis_index("level"), lax.axis_index("row"), lax.axis_index("col")
+
+    def place(level):
+        return jnp.where(level == 7, 5, jnp.where(level == 5, 3, jnp.where(level == 3, 7, level)))
+
+    l = jnp.where(p == 5, 7, jnp.where(p == 3, 5, jnp.where(p == 7, 3, p)))
+    moved = l != p
     side, width = sides_ref.shape
     rows = width // chunks
     unit = rows // ncol
@@ -36,7 +42,7 @@
     others = [lax.rem(c + o, ncol) for o in range(1, ncol)]
     after, before = others[0], others[-1]
     split_from = whole_from - 1
-    up, down = lax.rem(l + 1, last), lax.rem(l + last - 1, last)
+    up, down = place(l + 1), place(l - 1)
 
     loads = [
         pltpu.make_async_copy(src, dst, load_sem.at[n])
@@ -59,34 +65,47 @@
 
     barrier = pltpu.get_barrier_semaphore()
     for o in others:
-        pl.semaphore_signal(barrier, inc=1, device_id=(l, z, o), device_id_type=MESH)
+        pl.semaphore_signal(barrier, inc=1, device_id=(p, z, o), device_id_type=MESH)
 
     @pl.when(l < last)
     def _():
         for q in range(nrow):
             pl.semaphore_signal(barrier, inc=1, device_id=(up, q, c), device_id_type=MESH)
+
+    @pl.when(l > 0)
+    def _():
+        for q in range(nrow):
             pl.semaphore_signal(barrier, inc=1, device_id=(down, q, c), device_id_type=MESH)
 
-    @pl.when(l == 0)
-    def _():
-        pl.semaphore_signal(barrier, inc=1, device_id=(last, z, c), device_id_type=MESH)
-
-    @pl.when(l == last)
-    def _():
-        pl.semaphore_signal(barrier, inc=1, device_id=(0, z, c), device_id_type=MESH)
+    @pl.when(moved)
+    def _():
+        pl.semaphore_signal(barrier, inc=1, device_id=(place(p), z, c), device_id_type=MESH)
+        pl.semaphore_signal(barrier, inc=1, device_id=(l, z, c), device_id_type=MESH)
+
+    @pl.when(p == 2)
+    def _():
+        pl.semaphore_signal(barrier, inc=1, device_id=(3, z, c), device_id_type=MESH)
+
+    @pl.when(p == 3)
+    def _():
+        pl.semaphore_signal(barrier, inc=1, device_id=(2, z, c), device_id_type=MESH)
 
     loads[0].wait()
     turned = sides_ref[...].T
     for o in range(ncol):
-        sides_row[o] = turned[o * rows:(o + 1) * rows]
+        home_sides[o] = turned[o * rows:(o + 1) * rows]
     loads[1].wait()
-    inv[c] = inverse_ref[...]
-    inv_t[c] = inverse_ref[...].T
+
+    @pl.when(jnp.logical_not(moved))
+    def _():
+        sides_row[...] = home_sides[...]
+        inv[c] = inverse_ref[...]
+
     update[...] = jnp.zeros_like(update)
     loads[2].wait()
     loads[3].wait()
 
-    @pl.when(l > 0)
+    @pl.when(p > 0)
     def _():
         def prepare(slot, carry):
             q = z + slot - BAND
@@ -95,22 +114,29 @@
             def _():
                 for a in range(ncol):
                     present = mask_ref[a, q].astype(f32)
-                    tile = tiles_ref[a, q] * present.astype(bf16)
-                    wb[slot, c, a * side:(a + 1) * side, :] = tile
-                    wt[slot, c, :, a * side:(a + 1) * side] = tile.T
+                    home_wb[slot, a * side:(a + 1) * side, :] = (
+                        tiles_ref[a, q] * present.astype(bf16))
 
             @pl.when((q < 0) | (q >= nrow))
             def _():
-                wb[slot, c] = jnp.zeros((ncol * side, side), bf16)
-                wt[slot, c] = jnp.zeros((side, ncol * side), bf16)
+                home_wb[slot] = jnp.zeros((ncol * side, side), bf16)
+
+            @pl.when(jnp.logical_not(moved))
+            def _():
+                wb[slot, c] = home_wb[slot]
+                for a in range(ncol):
+                    at = slice(a * side, (a + 1) * side)
+                    wt[slot, c, :, at] = home_wb[slot, at, :].T
             return carry
         lax.fori_loop(0, SLOTS, prepare, 0)
 
     pl.semaphore_wait(
         barrier,
         (ncol - 1)
-        + jnp.where(l < last, 2 * nrow, 1)
-        + jnp.where(l == 0, 1, 0),
+        + jnp.where(l < last, nrow, 0)
+        + jnp.where(l > 0, nrow, 0)
+        + jnp.where(moved, 2, 0)
+        + jnp.where((p == 2) | (p == 3), 1, 0),
     )
 
     def remote(src, dst, send, recv, device):
@@ -132,10 +158,10 @@
 
     def part_copy(k, o):
         return remote(
-            part.at[k, o], yin.at[k, c], fy_send.at[k, o], fy_recv.at[k, c], (l, z, o))
+            part.at[k, o], yin.at[k, c], fy_send.at[k, o], fy_recv.at[k, c], (p, z, o))
 
     def turn_copy(src, dst, send, recv, o):
-        return remote(src.at[o], dst.at[c], send.at[o], recv.at[c], (l, z, o))
+        return remote(src.at[o], dst.at[c], send.at[o], recv.at[c], (p, z, o))
 
     def turn_start(src, dst, send, recv):
         for o in others:
@@ -151,14 +177,14 @@
             turn_copy(src, dst, send, recv, o).wait_send()
 
     def inverse_copy(o):
-        return remote(inv.at[c], inv.at[c], d_send.at[o], d_recv.at[c], (l, z, o))
+        return remote(inv.at[c], inv.at[c], d_send.at[o], d_recv.at[c], (p, z, o))
 
     low, high = pl.ds(0, HALF), pl.ds(HALF, SLOTS - HALF)
 
     def bulk_copy(slots, owner, n, device):
         return remote(
             wb.at[slots, owner], wb.at[slots, owner], bulk_send.at[n], bulk_recv.at[n],
-            (l, z, device))
+            (p, z, device))
 
     def bulk_own():
         return [
@@ -171,15 +197,18 @@
 
     opposite = others[1]
 
+    def transpose_slab(owner):
+        def one(slot, carry):
+            for a in range(ncol):
+                at = slice(a * side, (a + 1) * side)
+                wt[slot, owner, :, at] = wb[slot, owner, at, :].T
+            return carry
+        lax.fori_loop(0, SLOTS, one, 0)
+
     def transpose_tiles(owner):
-        @pl.when((l >= whole_from) | (l == 0))
-        def _():
-            def one(slot, carry):
-                for a in range(ncol):
-                    at = slice(a * side, (a + 1) * side)
-                    wt[slot, owner, :, at] = wb[slot, owner, at, :].T
-                return carry
-            lax.fori_loop(0, SLOTS, one, 0)
+        @pl.when(l >= whole_from)
+        def _():
+            transpose_slab(owner)
 
     def spread_start():
         for copy in bulk_own():
@@ -206,16 +235,12 @@
 
     def ship_out():
         return [
-            ship(1, sides_use, sides_guest, 0), ship(2, inv, inv_guest, 0),
-            ship(3, inv_t, inv_t_guest, 0),
-            ship(0, wb.at[:, c], wb.at[:, c], 0),
+            ship(1, home_sides, sides_row, place(p)), ship(2, inverse_ref, inv.at[c], place(p)),
+            ship(0, home_wb, wb.at[:, c], place(p)),
         ]
 
-    def ship_back_y():
-        return ship(4, yblock_guest, yblock, last)
-
-    def ship_back_x():
-        return ship(5, xblock_guest, xblock, last)
+    def ship_back():
+        return [ship(3, yfinal, yhome, l), ship(4, xfinal, xhome, l)]
 
     def go(device):
         pl.semaphore_signal(go_sem, inc=1, device_id=(device, z, c), device_id_type=MESH)
@@ -244,10 +269,12 @@
         return jnp.concatenate([wb[slot, o] for o in range(ncol)], axis=1)
 
     def send_forward(k):
-        for d in FAR_FIRST:
-            @pl.when(exists(d))
-            def _():
-                forward_copy(k, d).start()
+        @pl.when(l < last)
+        def _():
+            for d in FAR_FIRST:
+                @pl.when(exists(d))
+                def _():
+                    forward_copy(k, d).start()
 
     near = range(-BAND + 3, BAND - 2)
     middling = [-BAND + 2, BAND - 2, -BAND + 1, BAND - 1]
@@ -257,16 +284,19 @@
         for d in sorted(distances, key=abs):
             await_slot(buffer, sems, k, d)
 
+    def forward_product(k, distances):
+        await_slots(xin, fz_recv, k, distances)
+        wide = jnp.concatenate([xin[k, d + BAND] for d in distances], axis=1)
+        weights = jnp.concatenate([wt[d + BAND, c] for d in distances], axis=0)
+        return jnp.dot(wide, weights, preferred_element_type=f32)
+
+    def forward_near(k):
+        near_total[...] = forward_product(k, near)
+
     def forward_parts(k):
-        def product(distances):
-            wide = jnp.concatenate([xin[k, d + BAND] for d in distances], axis=1)
-            weights = jnp.concatenate([wt[d + BAND, c] for d in distances], axis=0)
-            return jnp.dot(wide, weights, preferred_element_type=f32)
-
-        total = 0.0
-        for distances in (near, middling, far):
-            await_slots(xin, fz_recv, k, distances)
-            total = total + product(distances)
+        total = near_total[...]
+        for distances in (middling, far):
+            total = total + forward_product(k, distances)
 
         @pl.when(l < split_from)
         def _():
@@ -369,13 +399,10 @@
 
         put(xstage, k, to_rows(wide.astype(f32)))
 
-    def guest_step(k, carry):
-        solved = solve_split(stacked(sides_guest, k) - whole_product(k), inv_t_guest, 0)
-        put(ysplit_guest, k, solved.astype(f32))
-        wide = solve_split(solved.astype(f32), inv_guest, 1)
+    def turn_round(k):
+        wide = solve_split(stacked(ysplit, k), inv, 1)
         backward_parts(k, wide)
-        put(xstage_guest, k, to_rows(wide.astype(f32)))
-        return carry
+        put(xstage, k, to_rows(wide.astype(f32)))
 
     def sent(copy_of):
         def one(k, carry):
@@ -387,29 +414,24 @@
         lax.fori_loop(0, chunks, one, 0)
 
     def middle():
-        @pl.when(l < last)
-        def _():
-            yblock[...] = ystage[...].astype(bf16)
-
-        @pl.when(l == last)
-        def _():
-            arrived(yblock, ship_recv.at[4])
-
+        yblock[...] = ystage[...].astype(bf16)
         turn_start(yblock, yturned, y_send, y_recv)
 
-        @pl.when((l == 1) | (l == 2))
-        def _():
+        @pl.when(l == 5)
+        def _():
+            spread_pass_on()
+            spread_end()
+            go(2)
+
+        @pl.when(l == 2)
+        def _():
+            go(3)
             pl.semaphore_wait(go_sem, 1)
 
-        @pl.when((l == 1) | (l == 2) | (l == 4))
+        @pl.when((l > 0) & (l < 5))
         def _():
             spread_start()
             spread_pass_on()
-            spread_end()
-
-        @pl.when(l == 3)
-        def _():
-            go(2)
             spread_end()
 
         @pl.when(l < last)
@@ -432,31 +454,20 @@
             for o in others:
                 arrived(inv.at[o], d_recv.at[o])
             ysplit[...] = yturned[...].astype(f32)
-            forward_ref[...] = yblock[...].reshape(width, side)
+            yfinal[...] = yblock[...].reshape(width, side)
 
         @pl.when(l >= split_from)
         def _():
-            forward_ref[...] = yturned[...].reshape(width, side)
-
-    def guest():
-        arrived(wb.at[:, c], ship_recv.at[0])
-        spread_start()
-        transpose_tiles(c)
-        spread_pass_on()
-        spread_end()
-        go(1)
-        arrived(sides_guest, ship_recv.at[1])
-        arrived(inv_guest, ship_recv.at[2])
-        arrived(inv_t_guest, ship_recv.at[3])
-        lax.fori_loop(0, chunks, guest_step, 0)
-        yblock_guest[...] = ysplit_guest[...].astype(bf16)
-        ship_back_y().start()
-        xblock_guest[...] = xstage_guest[...].astype(bf16)
-        ship_back_x().start()
-        sent(backward_copy)
-        ship_back_y().wait_send()
-        ship_back_x().wait_send()
-
+            yfinal[...] = yturned[...].reshape(width, side)
+
+    @pl.when(moved)
+    def _():
+        for copy in ship_out():
+            copy.start()
+        arrived(sides_row, ship_recv.at[1])
+        arrived(inv.at[c], ship_recv.at[2])
+
+    inv_t[c] = inv[c].T
     for o in others:
         inverse_copy(o).start()
 
@@ -473,71 +484,79 @@
             inv_t[o] = inv[o].T
         turn_sent(sides_row, sides_use, s_send, s_recv)
 
-    @pl.when(l == last)
-    def _():
-        for copy in ship_out():
-            copy.start()
-
-    @pl.when((l == 3) | ((l >= 5) & (l < last)))
+    @pl.when(moved)
+    def _():
+        arrived(wb.at[:, c], ship_recv.at[0])
+
+    @pl.when(l == 5)
+    def _():
+        pl.semaphore_wait(go_sem, 1)
+
+    @pl.when(l >= 5)
     def _():
         spread_start()
+
+    @pl.when(moved)
+    def _():
+        transpose_slab(c)
+
+    @pl.when(l > 5)
+    def _():
         spread_pass_on()
-
-    @pl.when((l >= 5) & (l < last))
-    def _():
         spread_end()
 
+    def step(t, carry):
+        def stage(k, wanted, work):
+            @pl.when((k >= 0) & (k < chunks) & wanted)
+            def _():
+                work(k)
+
+        by_parts = (l > 0) & (l < whole_from)
+        stage(t, by_parts, forward_near)
+        stage(t - 1, l < split_from, forward_row)
+        stage(t - 1, l >= split_from, forward_split)
+        stage(t - 1, l == last, turn_round)
+        stage(t, by_parts, forward_parts)
+        return carry
+
+    lax.fori_loop(0, chunks + 1, step, 0)
+
+    middle()
+
     @pl.when(l < last)
     def _():
-        def step(t, carry):
-            def stage(k, wanted, work):
-                @pl.when((k >= 0) & (k < chunks) & wanted)
-                def _():
-                    work(k)
-
-            stage(t, (l > 0) & (l < whole_from), forward_parts)
-            stage(t - 1, l < split_from, forward_row)
-            stage(t - 1, l >= split_from, forward_split)
-            return carry
-
-        lax.fori_loop(0, chunks + 1, step, 0)
-
-    middle()
-
-    @pl.when(l == 0)
-    def _():
-        guest()
-
-    @pl.when(l < last)
-    def _():
         lax.fori_loop(0, chunks, lambda k, x: (backward_step(k), x)[1], 0)
-        xblock[...] = xstage[...].astype(bf16)
-
-    @pl.when(l == last)
-    def _():
-        arrived(xblock, ship_recv.at[5])
-
+
+    xblock[...] = xstage[...].astype(bf16)
     turn_start(xblock, xturned, x_send, x_recv)
     for o in others:
         inverse_copy(o).wait_send()
 
-    @pl.when((l > 0) & (l < last))
+    @pl.when(l > 0)
     def _():
         sent(backward_copy)
-
-    @pl.when(l < last)
-    def _():
         for copy in (*bulk_own(), *bulk_passed()):
             copy.wait_send()
 
-    @pl.when(l == last)
-    def _():
-        for copy in ship_out():
+    turn_arrived(xturned, x_recv)
+    xfinal[...] = xturned[...].reshape(width, side)
+    turn_sent(xblock, xturned, x_send, x_recv)
+
+    @pl.when(moved)
+    def _():
+        for copy in ship_back():
+            copy.start()
+        for copy in (*ship_out(), *ship_back()):
             copy.wait_send()
-
-    turn_arrived(xturned, x_recv)
-    answer_ref[...] = xturned[...].reshape(width, side)
-    turn_sent(xblock, xturned, x_send, x_recv)
+        arrived(yhome, ship_recv.at[3])
+        arrived(xhome, ship_recv.at[4])
+        forward_ref[...] = yhome[...]
+        answer_ref[...] = xhome[...]
+
+    @pl.when(jnp.logical_not(moved))
+    def _():
+        forward_ref[...] = yfinal[...]
+        answer_ref[...] = xfinal[...]
 
 
 def upright(forward_ref, answer_ref, forward_out, answer_out):
@@ -560,7 +579,7 @@
     dma = pltpu.SemaphoreType.DMA
     blocks = (ncol, rows, side)
     forward, answer = pl.pallas_call(
-        functools.partial(kernel, nlev, nrow, ncol, chunks, nlev - 3),
+        functools.partial(kernel, nlev, nrow, ncol, chunks, nlev - 2),
         name="levels",
         out_shape=[jax.ShapeDtypeStruct((width, side), bf16)] * 2,
         in_specs=[hbm] * 4,
@@ -597,15 +616,12 @@
             dma((chunks, SLOTS)), dma((chunks, SLOTS)),
             dma((6,)), dma((6,)),
             *[dma((ncol,)) for _ in range(8)],
+            pltpu.VMEM((SLOTS, ncol * side, side), bf16),
             pltpu.VMEM(blocks, f32),
-            pltpu.VMEM((ncol, side, side), bf16),
-            pltpu.VMEM((ncol, side, side), bf16),
-            pltpu.VMEM(blocks, f32),
-            pltpu.VMEM(blocks, f32),
-            pltpu.VMEM(blocks, bf16),
-            pltpu.VMEM(blocks, bf16),
-            dma((6,)), dma((6,)),
+            *[pltpu.VMEM((width, side), bf16) for _ in range(4)],
+            dma((5,)), dma((5,)),
             pltpu.SemaphoreType.REGULAR,
+            pltpu.VMEM((rows, ncol * side), f32),
         ],
         compiler_params=pltpu.CompilerParams(
             collective_id=0, has_side_effects=True, vmem_limit_bytes=60 * 2**20),

time: 181 us -> 175 us (0.967)
  Pallas kernels: 180 us -> 175 us
    pallas_call x1, Pallas kernels: 179 us -> 173 us  [local(): pl.pallas_call(functools.partial(kernel, nlev, nrow, ncol, chunks, nlev -...]
where the time goes in v5:
time: 175 us
  Pallas kernels  175 us (100%)
    pallas_call x1, Pallas kernels, local(): pl.pallas_call(functools.partial(kernel, nlev, nrow, ncol, chunks, nlev -...  173 us

profile of v5, /device:TPU:32, one launch (start us, length us, event | category | flops | bytes accessed | tf_op | source)
XLA Modules:
  0.0 175.2 jit_solution(671054442526891423)
XLA Ops:
  0.6 173.1 %levels.1 = (bf16[128,128]{1,0:T(8,128)(2,1)}, bf16[128,128]{1,0:T(8,128)(2,1)}) custom-call(bf16[4,16,128,128]{3,2,1,0:T(8,128)(2,1)} %bitcast.6, s32[4,16]{1,0:T(4,128)} %bitcast.11, bf16[128,128]{1,0:T(8,128)(2,1)} %bitcast.8, f32[128,128]{1,0:T(8,128)} %bitcast.7), custom_call_target="tpu_custom_call" | custom-call | flops 1073741824 | bytes 4194304 | tf_op jit(solution)/shard_map/levels/pallas_call | solution.py:581
  173.7 1.5 upright.1
